TPU v7x, 256 devices: a whole 4x4x8 slice. The times are simulated.
256 devices in a mesh: ctx: 32 (over z, x), head: 8 (over y, core).
Axes of the slice: x: 4, y: 4, z: 8, core: 2. Of those that a mesh axis runs over, the one named last changes fastest.
Arguments:
- query: bfloat16 [32768, 4096], P(('ctx', 'head')), may hold values from -90 to 90
- keys: bfloat16 [32768, 4096], P(('ctx', 'head')), may hold values from -4.5 to 4.5
- values: bfloat16 [32768, 4096], P(('ctx', 'head')), may hold values from -5 to 5
- grad_out: bfloat16 [32768, 4096], P(('ctx', 'head')), may hold values from -5 to 5
- random_owner: int32 [256, 3], replicated, may hold values from 0 to 31, all different within a row; in each aligned block of 8 rows (0 to 7, 8 to 15, ...) no two rows name the same one
- random_within: int32 [256, 3], replicated, may hold values from 0 to 7
- global_ids: int32 [256, 2], replicated, may hold values from 0 to 3, all different within a row
Outputs:
- grad_query: bfloat16 [32768, 4096], P(('ctx', 'head'))
- grad_keys: bfloat16 [32768, 4096], P(('ctx', 'head'))
- grad_values: bfloat16 [32768, 4096], P(('ctx', 'head'))
Inputs may be any that keep to these rules, and one draw needn't show every extreme that they name: `random_owner`: in the 8 rows of one index of ctx no owner is named more than 1 times, a bound that some block reaches in some of them; the 3 owners of one row differ. `global_ids`: the 2 blocks of one row differ; every block 0 to 3 is named by some row.
All inputs are finite; a program needn't handle non-finite values.
Results may differ from a plain program's by a relative error of at most 0.0053.
Values may be sent and summed in bfloat16 or wider, within the bound.
No kernel may reach another device: no remote copies, remote signals or barrier semaphores. Data moves between devices by JAX's collectives and lax.ppermute only.
A program may use at most 192 MiB of HBM per device.

v0:
```python
from functools import partial

import jax
import jax.numpy as jnp
from jax import lax
from jax.sharding import PartitionSpec as P

HEAD_DIM = 128
BLOCK = 128
RAND = 3
GLOB = 2
NGLOB = 4


def extended(cells, sides, width):
    for axis, dim in sides:
        count = lax.axis_size(axis)
        ends = count - 1
        head = lax.slice_in_dim(cells, 0, width, axis=dim)
        tail = lax.slice_in_dim(cells, cells.shape[dim] - width, cells.shape[dim], axis=dim)
        cells = jnp.concatenate(
            [
                lax.ppermute(tail, axis, [(i, (i + 1) % count) for i in range(ends)]),
                cells,
                lax.ppermute(head, axis, [((i + 1) % count, i) for i in range(ends)]),
            ],
            axis=dim,
        )
    return cells


def broadcast(block, axis, holder):
    block = jnp.where(lax.axis_index(axis) == holder, block, jnp.zeros_like(block))
    return lax.psum(block, axis)


def passed_along(block, axis, distance):
    devices = range(lax.axis_size(axis))
    route = [(i - distance, i) for i in devices if i - distance in devices]
    return lax.ppermute(block, axis, route)


def expand_to(mask, rank):
    return mask.reshape(mask.shape + (1,) * (rank - mask.ndim))


def block_grads(query_blocks, grad_blocks, key_values, slot_mask, score_scale, kept_slots):
    keys_part = key_values[:, 0]
    values_part = key_values[:, 1]
    scores = (
        jnp.einsum("bhqd,bhnkd->bhqnk", query_blocks, keys_part, preferred_element_type=jnp.float32)
        * score_scale
    )
    scores = jnp.where(slot_mask[:, None, None, :, None], scores, -jnp.inf)
    highest = jnp.max(scores, axis=(3, 4), keepdims=True)
    logsum = highest + jnp.log(jnp.sum(jnp.exp(scores - highest), axis=(3, 4), keepdims=True))
    probs = jnp.exp(scores - logsum)
    probs_low = probs.astype(jnp.bfloat16)
    dprobs = jnp.einsum(
        "bhqd,bhnkd->bhqnk", grad_blocks, values_part, preferred_element_type=jnp.float32
    )
    row_dot = jnp.sum(probs * dprobs, axis=(3, 4), keepdims=True)
    dscores = (probs * (dprobs - row_dot)).astype(jnp.bfloat16)
    grad_query = (
        jnp.einsum("bhqnk,bhnkd->bhqd", dscores, keys_part, preferred_element_type=jnp.float32)
        * score_scale
    )
    key_terms = (
        jnp.einsum("bhqnk,bhqd->bhnkd", dscores, query_blocks, preferred_element_type=jnp.float32)
        * score_scale
    )
    value_terms = jnp.einsum(
        "bhqnk,bhqd->bhnkd", probs_low, grad_blocks, preferred_element_type=jnp.float32
    )
    return (
        grad_query,
        jnp.stack([key_terms, value_terms], 1),
        logsum[..., 0, 0],
        row_dot[..., 0, 0],
    )


def on_device(query, keys, values, grad_out, random_owner, random_within, global_ids):
    ctx_count = lax.axis_size("ctx")
    head_count = lax.axis_size("head")
    ctx_index = lax.axis_index("ctx")
    tokens_in, width_all = query.shape
    features = width_all // head_count
    heads_dev = features // HEAD_DIM
    local_rows = tokens_in * head_count
    blocks = local_rows // BLOCK
    score_scale = HEAD_DIM ** (-0.5)
    unit_shape = (blocks, BLOCK, heads_dev, HEAD_DIM)
    query_split = query.reshape(tokens_in, head_count, features)
    keys_split = keys.reshape(tokens_in, head_count, features)
    values_split = values.reshape(tokens_in, head_count, features)
    grad_split = grad_out.reshape(tokens_in, head_count, features)
    spread = (
        lax.all_to_all(query_split, "head", split_axis=1, concat_axis=0, tiled=True),
        lax.all_to_all(keys_split, "head", split_axis=1, concat_axis=0, tiled=True),
        lax.all_to_all(values_split, "head", split_axis=1, concat_axis=0, tiled=True),
        lax.all_to_all(grad_split, "head", split_axis=1, concat_axis=0, tiled=True),
    )
    query_local = spread[0].reshape(unit_shape).transpose(0, 2, 1, 3)
    keys_local = spread[1].reshape(unit_shape).transpose(0, 2, 1, 3)
    values_local = spread[2].reshape(unit_shape).transpose(0, 2, 1, 3)
    grad_local = spread[3].reshape(unit_shape).transpose(0, 2, 1, 3)
    kv_local = jnp.stack([keys_local, values_local], 1)
    padded_kv = extended(kv_local, (("ctx", 0),), 1)
    summary_kv = broadcast(kv_local[:NGLOB], "ctx", 0)
    entries = blocks * RAND
    owner_all = random_owner.reshape(ctx_count, entries)
    within_all = random_within.reshape(ctx_count, entries)
    entry_ids = jnp.arange(entries, dtype=jnp.int32)
    earlier = entry_ids[None, :] < entry_ids[:, None]
    same_owner = owner_all[:, :, None] == owner_all[:, None, :]
    rank_all = jnp.sum(same_owner & earlier[None], axis=2)
    capacity = max(1, (4 * blocks * RAND + 3 * ctx_count - 1) // (3 * ctx_count))
    slot_ids = jnp.arange(capacity, dtype=jnp.int32)
    owned = owner_all == ctx_index
    hit = owned[:, :, None] & (rank_all[:, :, None] == slot_ids[None, None, :])
    own_index = jnp.sum(jnp.where(hit, within_all[:, :, None], 0), axis=1)
    own_valid = jnp.any(hit, axis=1)
    outgoing = jnp.where(expand_to(own_valid, 6), kv_local[own_index], jnp.zeros((), jnp.bfloat16))
    owner_mine = lax.dynamic_index_in_dim(owner_all, ctx_index, 0, keepdims=False)
    rank_mine = lax.dynamic_index_in_dim(rank_all, ctx_index, 0, keepdims=False)
    take_index = owner_mine * capacity + rank_mine
    take_bool = take_index[:, None] == jnp.arange(ctx_count * capacity, dtype=jnp.int32)[None, :]
    entry_of_slot = jnp.sum(jnp.where(take_bool, entry_ids[:, None], 0), axis=0)
    slot_used = jnp.any(take_bool, axis=0)
    incoming = lax.all_to_all(outgoing, "ctx", split_axis=0, concat_axis=0, tiled=True)
    incoming_flat = incoming.reshape((ctx_count * capacity,) + incoming.shape[2:])
    random_kv = (
        incoming_flat[take_index]
        .reshape((blocks, RAND) + incoming.shape[2:])
        .transpose(0, 2, 3, 1, 4, 5)
    )
    global_mine = lax.dynamic_slice_in_dim(global_ids, ctx_index * blocks, blocks, 0)
    global_kv = summary_kv[global_mine].transpose(0, 2, 3, 1, 4, 5)
    all_kv = jnp.concatenate(
        [
            padded_kv[:blocks, :, :, None],
            padded_kv[1 : blocks + 1, :, :, None],
            padded_kv[2:, :, :, None],
            global_kv,
            random_kv,
        ],
        axis=3,
    )
    block_ids = jnp.arange(blocks, dtype=jnp.int32)
    position = ctx_index * blocks + block_ids
    slot_mask = jnp.concatenate(
        [
            (position > 0)[:, None],
            jnp.ones((blocks, 1), bool),
            (position < ctx_count * blocks - 1)[:, None],
            jnp.ones((blocks, GLOB + RAND), bool),
        ],
        axis=1,
    )
    kept_slots = 3 + GLOB + RAND
    group_size = 4
    group_count = blocks // group_size
    grads_fn = partial(block_grads, score_scale=score_scale, kept_slots=kept_slots)

    def run_group(group_args):
        return grads_fn(*group_args)

    head_shape = query_local.shape[1:]
    grouped = (
        query_local.reshape((group_count, group_size) + head_shape),
        grad_local.reshape((group_count, group_size) + head_shape),
        all_kv.reshape((group_count, group_size) + all_kv.shape[1:]),
        slot_mask.reshape(group_count, group_size, slot_mask.shape[1]),
    )
    grad_query, slot_terms, logsum, row_dot = lax.map(run_group, grouped)
    grad_query = grad_query.reshape((blocks,) + head_shape)
    slot_terms = slot_terms.reshape((blocks,) + slot_terms.shape[2:])
    logsum = logsum.reshape((blocks,) + logsum.shape[2:])
    row_dot = row_dot.reshape((blocks,) + row_dot.shape[2:])
    no_pad = ((0, 0),) * 4
    padded_sum = jnp.pad(slot_terms[:, :, :, 0], ((0, 2),) + no_pad)
    padded_sum = padded_sum + jnp.pad(slot_terms[:, :, :, 1], ((1, 1),) + no_pad)
    padded_sum = padded_sum + jnp.pad(slot_terms[:, :, :, 2], ((2, 0),) + no_pad)
    from_right = passed_along(padded_sum[0], "ctx", -1)
    from_left = passed_along(padded_sum[blocks + 1].astype(jnp.bfloat16), "ctx", 1).astype(
        jnp.float32
    )
    key_total = padded_sum[1 : blocks + 1]
    key_total = key_total.at[blocks - 1].add(from_right)
    key_total = key_total.at[0].add(from_left)
    global_bool = (global_mine[:, :, None] == jnp.arange(NGLOB)[None, None, :]).astype(jnp.float32)
    global_terms = jnp.einsum(
        "bgn,bxhgkd->nxhkd",
        global_bool,
        slot_terms[:, :, :, 3 : 3 + GLOB],
        precision=lax.Precision.HIGHEST,
    )
    global_sum = lax.psum(global_terms, "ctx")
    key_total = key_total.at[:NGLOB].add(jnp.where(ctx_index == 0, global_sum, 0.0))
    term_shape = key_total.shape[1:]
    random_terms = (
        jnp.moveaxis(slot_terms[:, :, :, 3 + GLOB :], 3, 1)
        .reshape((entries,) + term_shape)
        .astype(jnp.bfloat16)
    )
    back_terms = jnp.where(
        expand_to(slot_used, 5), random_terms[entry_of_slot], jnp.zeros((), jnp.bfloat16)
    )
    back_terms = back_terms.reshape((ctx_count, capacity) + term_shape)
    returned = lax.all_to_all(back_terms, "ctx", split_axis=0, concat_axis=0, tiled=True)
    returned = jnp.where(expand_to(own_valid, 6), returned.astype(jnp.float32), 0.0)
    key_total = key_total.at[own_index.reshape(-1)].add(
        returned.reshape((ctx_count * capacity,) + term_shape)
    )
    query_back = (
        grad_query.transpose(0, 2, 1, 3).reshape(local_rows, 1, features).astype(jnp.bfloat16)
    )
    keys_back = (
        key_total[:, 0].transpose(0, 2, 1, 3).reshape(local_rows, 1, features).astype(jnp.bfloat16)
    )
    values_back = (
        key_total[:, 1].transpose(0, 2, 1, 3).reshape(local_rows, 1, features).astype(jnp.bfloat16)
    )
    gathered = (
        lax.all_to_all(query_back, "head", split_axis=0, concat_axis=1, tiled=True),
        lax.all_to_all(keys_back, "head", split_axis=0, concat_axis=1, tiled=True),
        lax.all_to_all(values_back, "head", split_axis=0, concat_axis=1, tiled=True),
    )
    grad_query_out = gathered[0].reshape(tokens_in, width_all)
    grad_keys_out = gathered[1].reshape(tokens_in, width_all)
    grad_values_out = gathered[2].reshape(tokens_in, width_all)
    return (grad_query_out, grad_keys_out, grad_values_out)


def solution(mesh):
    return jax.shard_map(
        on_device,
        mesh=mesh,
        in_specs=(
            P(("ctx", "head"), None),
            P(("ctx", "head"), None),
            P(("ctx", "head"), None),
            P(("ctx", "head"), None),
            P(),
            P(),
            P(),
        ),
        out_specs=(P(("ctx", "head"), None), P(("ctx", "head"), None), P(("ctx", "head"), None)),
        check_vma=False,
    )
```

profile of v0, /device:TPU:102, one launch (start us, length us, event | category | flops | bytes accessed | tf_op | source)
XLA Modules:
  0.0 874.7 jit_solution(11515931746888695809)
XLA Ops:
  9.6 4.5 all-to-all-start.2
  16.3 13.7 %all-to-all-done.2 = bf16[128,8,512]{0,2,1:T(8,128)(2,1)S(1)} async-done(((bf16[128,8,512]{0,2,1:T(8,128)(2,1)}), bf16[128,8,512]{0,2,1:T(8,128)(2,1)S(1)}, u32[]{:S(2)}, u32[]{:S(2)}) %all-to-all-start.2) | async-done | bytes 1048608 | tf_op jit(solution)/shard_map/all_to_all | solution.py:101
  30.0 3.6 all-to-all-start.1
  37.8 11.7 %all-to-all-done.1 = bf16[128,8,512]{0,2,1:T(8,128)(2,1)S(1)} async-done(((bf16[128,8,512]{0,2,1:T(8,128)(2,1)}), bf16[128,8,512]{0,2,1:T(8,128)(2,1)S(1)}, u32[]{:S(2)}, u32[]{:S(2)}) %all-to-all-start.1) | async-done | bytes 1048608 | tf_op jit(solution)/shard_map/all_to_all | solution.py:100
  49.4 3.6 all-to-all-start
  56.1 2.8 collective-permute-start.1
  58.8 6.4 collective-permute-start
  65.3 10.2 %collective-permute-done.1 = bf16[1,2,4,128,128]{4,0,3,2,1:T(2,128)(2,1)S(1)} collective-permute-done((bf16[1,2,4,128,128]{4,0,3,2,1:T(2,128)(2,1)S(1)}, bf16[1,2,4,128,128]{4,0,3,2,1:T(2,128)(2,1)S(1)}, u32[]{:S(2)}, u32[]{:S(2)}) %collective-permute-start.1) | collective-permute-done | bytes 262176 | tf_op jit(solution)/shard_map/ppermute | solution.py:25
  76.7 3.5 pad_maximum_fusion
  80.7 4.9 gather_fusion.1
  85.7 7.2 fusion.35
  92.9 10.7 %all-to-all-start.3 = ((bf16[32,1,2,4,128,128]{5,4,3,2,1,0:T(8,128)(2,1)}), bf16[32,1,2,4,128,128]{5,4,3,2,1,0:T(8,128)(2,1)}, u32[]{:S(2)}, u32[]{:S(2)}) async-start(bf16[32,1,2,4,128,128]{5,4,3,2,1,0:T(8,128)(2,1)} %fusion.35), calls=%async_computation.3 | async-start | bytes 16777216 | tf_op jit(solution)/shard_map/all_to_all | solution.py:131
  111.6 3.5 copy_dynamic-update-slice_fusion.2
  115.1 189.4 %all-to-all-done.3 = bf16[32,1,2,4,128,128]{5,4,3,2,1,0:T(8,128)(2,1)} async-done(((bf16[32,1,2,4,128,128]{5,4,3,2,1,0:T(8,128)(2,1)}), bf16[32,1,2,4,128,128]{5,4,3,2,1,0:T(8,128)(2,1)}, u32[]{:S(2)}, u32[]{:S(2)}) %all-to-all-start.3) | async-done | bytes 8388640 | tf_op jit(solution)/shard_map/all_to_all | solution.py:131
  304.5 4.9 all-to-all-start.4
  309.4 3.1 maximum_dynamic-update-slice_fusion
  312.5 3.4 copy_dynamic-update-slice_fusion.1
  315.9 17.0 %all-reduce.6.cloned.1.call-done = bf16[4,2,4,128,128]{4,0,3,2,1:T(4,128)(2,1)} async-done(((bf16[4,2,4,128,128]{4,0,3,2,1:T(4,128)(2,1)}), bf16[4,2,4,128,128]{4,0,3,2,1:T(4,128)(2,1)}) %all-reduce.6.cloned.1.call-update) | async-done | bytes 1048592 | tf_op jit(solution)/shard_map/psum | solution.py:34
  334.4 3.0 gather_fusion
  339.9 2.8 constant_dynamic-update-slice_fusion.1
  342.7 7.9 gather_fusion.2
  350.6 4.1 copy.260
  354.7 4.0 constant_dynamic-update-slice_fusion
  358.7 89.0 %while.15 = (s32[]{:T(128)}, bf16[2,4,4,128,128]{4,3,2,1,0:T(8,128)(2,1)}, f32[2,4,2,4,8,128,128]{6,1,0,4,5,3,2:T(4,128)}, pred[2,4,8]{2,1,0:T(4,128)(4,1)S(1)},...) while((s32[]{:T(128)}, ...), condition=%wide.region_10.11_spmd, body=%wide.region_6.10_spmd.sunk | while | flops 2737041408 | bytes 196175664 | solution.py:176
  358.8 10.3 %copy_bitcast_fusion.3 = bf16[4,2,4,8,128,128]{5,4,3,2,0,1:T(8,128)(2,1)} fusion(bf16[2,4,2,4,8,128,128]{6,5,4,3,2,1,0:T(8,128)(2,1)} %get-tuple-element.246, s32[]{:T(128)S(6)} %copy.334), kind=kLoop, calls=%fused_computation.7.clone.1 | loop fusion | bytes 16777220 | tf_op jit(solution)/shard_map/while/body/jit(dynamic_index_in_dim)/squeeze | solution.py:176
  369.2 3.1 fusion.72
  374.1 4.2 multiply_reduce_fusion.2
  380.8 3.8 fusion.73
  390.7 12.4 %copy_dynamic-update-slice_fusion.4 = f32[2,4,2,4,8,128,128]{6,1,0,4,5,3,2:T(4,128)} fusion(f32[2,4,2,4,8,128,128]{6,1,0,4,5,3,2:T(4,128)} %get-tuple-element.235, s32[]{:T(128)S(6)} %copy.334, f32[1,4,2,4,8,128,128]{6,5,4,3,1,2,0:T(8,128)S(1)} %maximum_bitcast_fusion.2), kind=kLoop, calls=%fused_computation.6.clone.1 | loop fusion | bytes 33554436 | tf_op jit(solution)/shard_map/while/body/jit(dynamic_update_index_in_dim)/dynamic_update_slice | solution.py:176
  403.1 10.3 %copy_bitcast_fusion.3 = bf16[4,2,4,8,128,128]{5,4,3,2,0,1:T(8,128)(2,1)} fusion(bf16[2,4,2,4,8,128,128]{6,5,4,3,2,1,0:T(8,128)(2,1)} %get-tuple-element.246, s32[]{:T(128)S(6)} %copy.334), kind=kLoop, calls=%fused_computation.7.clone.1 | loop fusion | bytes 16777220 | tf_op jit(solution)/shard_map/while/body/jit(dynamic_index_in_dim)/squeeze | solution.py:176
  413.5 3.1 fusion.72
  418.4 4.2 multiply_reduce_fusion.2
  425.1 3.8 fusion.73
  435.0 12.3 %copy_dynamic-update-slice_fusion.4 = f32[2,4,2,4,8,128,128]{6,1,0,4,5,3,2:T(4,128)} fusion(f32[2,4,2,4,8,128,128]{6,1,0,4,5,3,2:T(4,128)} %get-tuple-element.235, s32[]{:T(128)S(6)} %copy.334, f32[1,4,2,4,8,128,128]{6,5,4,3,1,2,0:T(8,128)S(1)} %maximum_bitcast_fusion.2), kind=kLoop, calls=%fused_computation.6.clone.1 | loop fusion | bytes 33554436 | tf_op jit(solution)/shard_map/while/body/jit(dynamic_update_index_in_dim)/dynamic_update_slice | solution.py:176
  447.7 5.5 fusion.36
  453.2 4.3 copy.275
  457.5 7.9 gather_fusion.3
  465.4 7.2 fusion.34
  472.6 8.5 all-to-all-start.6
  481.2 8.6 fusion.38
  489.8 8.9 %slice_bitcast_fusion.15 = (f32[8,2,4,128,128]{4,0,3,2,1:T(8,128)S(1)}, f32[8,2,4,128,128]{4,0,3,2,1:T(8,128)}, f32[8,2,4,128,128]{4,0,3,2,1:T(8,128)}) fusion(f32[8,2,4,8,128,128]{5,0,3,4,2,1:T(8,128)} %bitcast.267), kind=kLoop, calls=%fused_computation.60 | loop fusion | bytes 25165824 | tf_op jit(solution)/shard_map/squeeze | solution.py:182
  498.7 4.3 pad_add_fusion
  504.7 2.8 collective-permute-start.2
  508.0 6.4 collective-permute-start.3
  522.1 165.8 %collective-permute-done.3 = bf16[2,4,128,128]{3,2,1,0:T(8,128)(2,1)} collective-permute-done((bf16[2,4,128,128]{3,2,1,0:T(8,128)(2,1)S(1)}, bf16[2,4,128,128]{3,2,1,0:T(8,128)(2,1)}, u32[]{:S(2)}, u32[]{:S(2)}) %collective-permute-start.3) | collective-permute-done | bytes 262176 | tf_op jit(solution)/shard_map/ppermute | solution.py:40
  688.9 11.7 %collective-permute-done.2 = f32[2,4,128,128]{3,2,1,0:T(8,128)S(1)} collective-permute-done((f32[2,4,128,128]{3,2,1,0:T(8,128)}, f32[2,4,128,128]{3,2,1,0:T(8,128)S(1)}, u32[]{:S(2)}, u32[]{:S(2)}) %collective-permute-start.2) | collective-permute-done | bytes 524320 | tf_op jit(solution)/shard_map/ppermute | solution.py:40
  700.6 15.2 %scatter-add.16 = f32[8,2,4,128,128]{4,0,3,2,1:T(8,128)} dynamic-update-slice(f32[8,2,4,128,128]{4,0,3,2,1:T(8,128)} %slice.193, f32[1,2,4,128,128]{4,0,3,2,1:T(1,128)S(1)} %bitcast.286, s32[]{:T(128)} %constant.148.clone.1, s32[]{:T(128)} %constant.136.clone.1, s32[]{:T(128)} %constant.136.clone.1, s32[]{:T(128)} %constant.136.clone.1, s32[]{:T(128)} %constant.136.clone.1) | dynamic-update-slice | bytes 1048580 | tf_op jit(solution)/shard_map/scatter-add | solution.py:190
  715.8 2.7 slice_add_fusion.1
  718.5 15.2 %scatter-add.19 = f32[8,2,4,128,128]{4,0,3,2,1:T(8,128)} dynamic-update-slice(f32[8,2,4,128,128]{4,0,3,2,1:T(8,128)} %scatter-add.16, f32[1,2,4,128,128]{4,0,3,2,1:T(1,128)S(1)} %slice_add_fusion.1, s32[]{:T(128)} %constant.136.clone.1, s32[]{:T(128)} %constant.136.clone.1, s32[]{:T(128)} %constant.136.clone.1, s32[]{:T(128)} %constant.136.clone.1, s32[]{:T(128)} %constant.136.clone.1) | dynamic-update-slice | bytes 1048580 | tf_op jit(solution)/shard_map/scatter-add | solution.py:191
  733.7 4.1 fusion.37
  737.8 4.9 copy.278
  742.7 4.3 all-to-all-start.5
  747.1 11.9 %select_bitcast_fusion = f32[32,2,4,128,128]{4,3,2,1,0:T(8,128)} fusion(bf16[32,1,2,4,128,128]{5,4,3,2,1,0:T(8,128)(2,1)} %all-to-all-done.6, pred[32]{0:T(512)(128)(4,1)S(1)} %copy-done.12), kind=kLoop, calls=%fused_computation.48 | loop fusion | flops 8388608 | bytes 25165856 | tf_op jit(solution)/shard_map/reshape | solution.py:214
  759.0 34.8 %scatter_fusion = f32[8,2,4,128,128]{4,3,2,1,0:T(8,128)} fusion(f32[8,2,4,128,128]{4,3,2,1,0:T(8,128)} %copy.278, s32[32]{0:T(128)S(1)} %fusion.53, f32[32,2,4,128,128]{4,3,2,1,0:T(8,128)} %select_bitcast_fusion), kind=kCustom, calls=%fused_computation.4 | custom fusion | flops 4194304 | bytes 50331776 | tf_op jit(solution)/shard_map/scatter-add | solution.py:213
  799.2 5.9 reshape.494
  805.1 8.0 reduce.16
  815.7 5.0 all-to-all-start.7
  820.7 3.0 copy.295
  823.7 5.9 reshape.495
  829.6 8.0 reduce.17
  840.2 4.8 all-to-all-start.8
  848.3 4.3 reshape.502
  854.9 6.2 all-to-all-done.8
  861.1 4.3 reshape.504
  (142 shorter events, 75.8 us)
Async XLA Ops:
  7.2 26.4 %copy-start.6 = (bf16[128,4096]{1,0:T(8,128)(2,1)S(1)}, bf16[128,4096]{1,0:T(8,128)(2,1)}, u32[]{:S(2)}) copy-start(bf16[128,4096]{1,0:T(8,128)(2,1)} %param.15) | copy-start | bytes 3145732
  7.2 27.7 %copy-start.10 = (s32[256,3]{0,1:T(4,128)S(1)}, s32[256,3]{0,1:T(4,128)}, u32[]{:S(2)}) copy-start(s32[256,3]{0,1:T(4,128)} %param.19) | copy-start | bytes 9220
  7.2 28.5 %copy-start.13 = (s32[256,3]{0,1:T(4,128)S(1)}, s32[256,3]{0,1:T(4,128)}, u32[]{:S(2)}) copy-start(s32[256,3]{0,1:T(4,128)} %param.20) | copy-start | bytes 9220
  7.2 28.8 %copy-start.16 = (s32[256,2]{0,1:T(2,128)S(1)}, s32[256,2]{0,1:T(2,128)}, u32[]{:S(2)}) copy-start(s32[256,2]{0,1:T(2,128)} %param.21) | copy-start | bytes 6148
  9.6 20.4 %all-to-all-start.2 = ((bf16[128,8,512]{0,2,1:T(8,128)(2,1)}), bf16[128,8,512]{0,2,1:T(8,128)(2,1)S(1)}, u32[]{:S(2)}, u32[]{:S(2)}) async-start(bf16[128,8,512]{0,2,1:T(8,128)(2,1)} %bitcast.30), calls=%async_computation.2 | async-start | bytes 2097152 | tf_op jit(solution)/shard_map/all_to_all | solution.py:101
  30.0 19.5 %all-to-all-start.1 = ((bf16[128,8,512]{0,2,1:T(8,128)(2,1)}), bf16[128,8,512]{0,2,1:T(8,128)(2,1)S(1)}, u32[]{:S(2)}, u32[]{:S(2)}) async-start(bf16[128,8,512]{0,2,1:T(8,128)(2,1)} %bitcast.24), calls=%async_computation.1 | async-start | bytes 2097152 | tf_op jit(solution)/shard_map/all_to_all | solution.py:100
  36.0 29.3 %copy-start.17 = (s32[32]{0:T(128)}, s32[32]{0:T(128)S(1)}, u32[]{:S(2)}) copy-start(s32[32]{0:T(128)S(1)} %reduce_sum.61) | copy-start | bytes 388
  37.0 48.6 %copy-start.11 = (pred[32]{0:T(512)(128)(4,1)}, pred[32]{0:T(512)(128)(4,1)S(1)}, u32[]{:S(2)}) copy-start(pred[32]{0:T(512)(128)(4,1)S(1)} %reduce_or.27) | copy-start | bytes 100
  37.8 42.4 %copy-start = (bf16[8,128,4,128]{3,0,1,2:T(8,128)(2,1)}, bf16[8,128,4,128]{3,0,1,2:T(8,128)(2,1)S(1)}, u32[]{:S(2)}) copy-start(bf16[8,128,4,128]{3,0,1,2:T(8,128)(2,1)S(1)} %copy.246) | copy-start | bytes 3145732
  49.4 3.6 copy-start.4
  49.4 43.4 %all-to-all-start = ((bf16[128,8,512]{0,2,1:T(8,128)(2,1)}), bf16[128,8,512]{0,2,1:T(8,128)(2,1)S(1)}, u32[]{:S(2)}, u32[]{:S(2)}) async-start(bf16[128,8,512]{0,2,1:T(8,128)(2,1)} %bitcast.18), calls=%async_computation | async-start | bytes 2097152 | tf_op jit(solution)/shard_map/all_to_all | solution.py:99
  54.7 25.5 %copy-start.2 = (bf16[8,128,4,128]{3,0,1,2:T(8,128)(2,1)}, bf16[8,128,4,128]{3,0,1,2:T(8,128)(2,1)S(1)}, u32[]{:S(2)}) copy-start(bf16[8,128,4,128]{3,0,1,2:T(8,128)(2,1)S(1)} %copy.244) | copy-start | bytes 3145732
  56.1 19.4 %collective-permute-start.1 = (bf16[1,2,4,128,128]{4,0,3,2,1:T(2,128)(2,1)S(1)}, bf16[1,2,4,128,128]{4,0,3,2,1:T(2,128)(2,1)S(1)}, u32[]{:S(2)}, u32[]{:S(2)}) collective-permute-start(bf16[1,2,4,128,128]{4,0,3,2,1:T(2,128)(2,1)S(1)} %get-tuple-element.168), channel_id=1, source_target_pairs={{8,0},{16,8},{24,16},{32,24},{40,32},{48,40},{56,48},{64,56},{72,6... | collective-permute-start | bytes 786440 | tf_op jit(solution)/shard_map/ppermute | solution.py:25
  58.8 17.8 %collective-permute-start = (bf16[1,2,4,128,128]{4,0,3,2,1:T(2,128)(2,1)S(1)}, bf16[1,2,4,128,128]{4,0,3,2,1:T(2,128)(2,1)S(1)}, u32[]{:S(2)}, u32[]{:S(2)}) collective-permute-start(bf16[1,2,4,128,128]{4,0,3,2,1:T(2,128)(2,1)S(1)} %get-tuple-element.169), channel_id=1, source_target_pairs={{0,8},{8,16},{16,24},{24,32},{32,40},{40,48},{48,56},{56,64},{64,7... | collective-permute-start | bytes 786440 | tf_op jit(solution)/shard_map/ppermute | solution.py:23
  92.9 14.8 %copy-start.1 = (bf16[8,128,4,128]{3,0,1,2:T(8,128)(2,1)S(1)}, bf16[8,128,4,128]{3,0,1,2:T(8,128)(2,1)}, u32[]{:S(2)}) copy-start(bf16[8,128,4,128]{3,0,1,2:T(8,128)(2,1)} %copy-done) | copy-start | bytes 3145732
  92.9 14.8 %copy-start.3 = (bf16[8,128,4,128]{3,0,1,2:T(8,128)(2,1)S(1)}, bf16[8,128,4,128]{3,0,1,2:T(8,128)(2,1)}, u32[]{:S(2)}) copy-start(bf16[8,128,4,128]{3,0,1,2:T(8,128)(2,1)} %copy-done.2) | copy-start | bytes 3145732
  92.9 211.6 %all-to-all-start.3 = ((bf16[32,1,2,4,128,128]{5,4,3,2,1,0:T(8,128)(2,1)}), bf16[32,1,2,4,128,128]{5,4,3,2,1,0:T(8,128)(2,1)}, u32[]{:S(2)}, u32[]{:S(2)}) async-start(bf16[32,1,2,4,128,128]{5,4,3,2,1,0:T(8,128)(2,1)} %fusion.35), calls=%async_computation.3 | async-start | bytes 16777216 | tf_op jit(solution)/shard_map/all_to_all | solution.py:131
  103.6 229.4 %all-reduce.6.cloned.1.call-start = ((), (), s32[]{:S(2)}) async-start(), calls=%async_computation.9 | async-start | bytes 2097152 | tf_op jit(solution)/shard_map/psum | solution.py:34
  110.4 199.0 %copy-start.5 = (bf16[2,4,1,4,1,128,128]{6,5,4,3,2,1,0:T(8,128)(2,1)S(1)}, bf16[2,4,1,4,1,128,128]{6,5,4,3,2,1,0:T(8,128)(2,1)}, u32[]{:S(2)}) copy-start(bf16[2,4,1,4,1,128,128]{6,5,4,3,2,1,0:T(8,128)(2,1)} %copy.248) | copy-start | bytes 3145732
  304.5 54.2 %all-to-all-start.4 = ((bf16[128,8,512]{0,2,1:T(8,128)(2,1)}), bf16[128,8,512]{0,2,1:T(8,128)(2,1)S(1)}, u32[]{:S(2)}, u32[]{:S(2)}) async-start(bf16[128,8,512]{0,2,1:T(8,128)(2,1)} %bitcast.275), calls=%async_computation.4 | async-start | bytes 2097152 | tf_op jit(solution)/shard_map/all_to_all | solution.py:102
  378.3 2.6 copy-start.7
  384.7 1.0 copy-start.8
  422.5 2.6 copy-start.7
  428.9 1.0 copy-start.8
  457.5 7.9 copy-start.15
  472.6 8.5 copy-start.14
  472.6 270.1 %all-to-all-start.6 = ((bf16[32,1,2,4,128,128]{5,4,3,2,1,0:T(8,128)(2,1)}), bf16[32,1,2,4,128,128]{5,4,3,2,1,0:T(8,128)(2,1)}, u32[]{:S(2)}, u32[]{:S(2)}) async-start(bf16[32,1,2,4,128,128]{5,4,3,2,1,0:T(8,128)(2,1)} %fusion.34), calls=%async_computation.6 | async-start | bytes 16777216 | tf_op jit(solution)/shard_map/all_to_all | solution.py:211
  481.1 252.6 %all-reduce.8.cloned.1.call-start = ((), (), s32[]{:S(2)}) async-start(), calls=%async_computation.10 | async-start | bytes 4194304 | tf_op jit(solution)/shard_map/psum | solution.py:199
  498.6 15.7 %copy-start.18 = (s32[32]{0:T(128)S(1)}, s32[32]{0:T(128)}, u32[]{:S(2)}) copy-start(s32[32]{0:T(128)} %copy-done.17) | copy-start | bytes 388
  503.0 13.8 %copy-start.9 = (bf16[2,4,4,128,128]{4,3,2,1,0:T(8,128)(2,1)S(1)}, bf16[2,4,4,128,128]{4,3,2,1,0:T(8,128)(2,1)}, u32[]{:S(2)}) copy-start(bf16[2,4,4,128,128]{4,3,2,1,0:T(8,128)(2,1)} %get-tuple-element.77) | copy-start | bytes 3145732
  504.7 195.9 %collective-permute-start.2 = (f32[2,4,128,128]{3,2,1,0:T(8,128)}, f32[2,4,128,128]{3,2,1,0:T(8,128)S(1)}, u32[]{:S(2)}, u32[]{:S(2)}) collective-permute-start(f32[2,4,128,128]{3,2,1,0:T(8,128)} %bitcast.66), channel_id=1, source_target_pairs={{8,0},{16,8},{24,16},{32,24},{40,32},{48,40},{56,48},{64,56},{72,6... | collective-permute-start | bytes 1572872 | tf_op jit(solution)/shard_map/ppermute | solution.py:40
  508.0 179.9 %collective-permute-start.3 = (bf16[2,4,128,128]{3,2,1,0:T(8,128)(2,1)S(1)}, bf16[2,4,128,128]{3,2,1,0:T(8,128)(2,1)}, u32[]{:S(2)}, u32[]{:S(2)}) collective-permute-start(bf16[2,4,128,128]{3,2,1,0:T(8,128)(2,1)S(1)} %bitcast.291), channel_id=1, source_target_pairs={{0,8},{8,16},{16,24},{24,32},{32,40},{40,48},{48,56},{56,64},{64,7... | collective-permute-start | bytes 786440 | tf_op jit(solution)/shard_map/ppermute | solution.py:40
  733.7 13.4 %copy-start.12 = (pred[32]{0:T(512)(128)(4,1)S(1)}, pred[32]{0:T(512)(128)(4,1)}, u32[]{:S(2)}) copy-start(pred[32]{0:T(512)(128)(4,1)} %copy-done.11) | copy-start | bytes 100
  742.7 73.0 %all-to-all-start.5 = ((bf16[8,2,32768]{2,1,0:T(2,128)(2,1)}), bf16[8,2,32768]{2,1,0:T(2,128)(2,1)S(1)}, u32[]{:S(2)}, u32[]{:S(2)}) async-start(bf16[8,2,32768]{2,1,0:T(2,128)(2,1)} %reshape.499), calls=%async_computation.5 | async-start | bytes 2097152 | tf_op jit(solution)/shard_map/all_to_all | solution.py:226
  815.7 24.5 %all-to-all-start.7 = ((bf16[8,2,32768]{2,1,0:T(2,128)(2,1)}), bf16[8,2,32768]{2,1,0:T(2,128)(2,1)}, u32[]{:S(2)}, u32[]{:S(2)}) async-start(bf16[8,2,32768]{2,1,0:T(2,128)(2,1)} %reshape.501), calls=%async_computation.7 | async-start | bytes 2097152 | tf_op jit(solution)/shard_map/all_to_all | solution.py:227
  840.2 20.9 %all-to-all-start.8 = ((bf16[8,2,32768]{2,1,0:T(2,128)(2,1)}), bf16[8,2,32768]{2,1,0:T(2,128)(2,1)}, u32[]{:S(2)}, u32[]{:S(2)}) async-start(bf16[8,2,32768]{2,1,0:T(2,128)(2,1)} %reshape.503), calls=%async_computation.8 | async-start | bytes 2097152 | tf_op jit(solution)/shard_map/all_to_all | solution.py:228
Sparse Core Ops, SparseCore 0:
  109.3 223.6 all-reduce.5
  489.9 209.4 all-reduce.7
where the time goes:
time: 884 us; the launch traced here: 875 us
  waiting for transfers between devices  427 us (48%)
  local copies, waits for them, and re-layouts  209 us (24%)
  other arithmetic  118 us (13%)
  starting transfers between devices  68.2 us (8%)
  matrix products  36.7 us (4%)
  between operations  14.9 us (2%)
    all_to_all x1, waiting for transfers between devices, on_device(): lax.all_to_all(outgoing, 'ctx', split_axis=0, concat_axis=0, tiled=True)  189 us
    ppermute x2, waiting for transfers between devices, passed_along(): return lax.ppermute(block, axis, route)  177 us
    unnamed x56, local copies, waits for them, and re-layouts  39.9 us
    scatter-add x1, other arithmetic, on_device(): key_total.at[own_index.reshape(-1)]  34.8 us
    dynamic_update_slice x2, local copies, waits for them, and re-layouts, on_device(): grad_query, slot_terms, logsum, row_dot = lax.map(run_group, grouped)  24.8 us
    squeeze x2, local copies, waits for them, and re-layouts, on_device(): grad_query, slot_terms, logsum, row_dot = lax.map(run_group, grouped)  20.7 us
  transfers between devices with their start and end apart: 15, of which 9 were waited for; matrix products, arithmetic and copies ran while one was open for 28% of the time, Pallas kernels for 0%

commit v1 on v0

v1 whole, which is shorter than its diff:
```python
from functools import partial

import jax
import jax.numpy as jnp
from jax import lax
from jax.experimental import pallas as pl
from jax.experimental.pallas import tpu as pltpu
from jax.sharding import Mesh, PartitionSpec as P

HEAD_DIM = 128
BLOCK = 128
RAND = 3
GLOB = 2
NGLOB = 4
NX = 4
SLOTS = 3 + GLOB
BF16 = jnp.bfloat16
F32 = jnp.float32
VMEM_LIMIT = 58 * 1024 * 1024
SCALE = HEAD_DIM ** (-0.5)
CTX = ("z", "x")


def dot_nt(a, b):
    return lax.dot_general(a, b, (((1,), (1,)), ((), ())), preferred_element_type=F32)


def dot_nn(a, b):
    return lax.dot_general(a, b, (((1,), (0,)), ((), ())), preferred_element_type=F32)


def dot_tn(a, b):
    return lax.dot_general(a, b, (((0,), (0,)), ((), ())), preferred_element_type=F32)


def params():
    return pltpu.CompilerParams(vmem_limit_bytes=VMEM_LIMIT)


def whole(shape):
    return pl.BlockSpec(shape, lambda *_: (0,) * len(shape))


def call(body, grid, scalars, ins, in_specs, out_shape, out_specs, scratch=()):
    return pl.pallas_call(
        body,
        grid_spec=pltpu.PrefetchScalarGridSpec(
            num_scalar_prefetch=len(scalars),
            grid=grid,
            in_specs=in_specs,
            out_specs=out_specs,
            scratch_shapes=list(scratch),
        ),
        out_shape=out_shape,
        compiler_params=params(),
    )(*scalars, *ins)


def pick_body(row_ref, x_ref, o_ref):
    o_ref[0] = x_ref[row_ref[pl.program_id(0)]]


def pick_rows(rows_of, x, count):
    block = (1,) + x.shape[1:]
    zeros = (0,) * (x.ndim - 1)
    return call(
        pick_body,
        (count,),
        (rows_of,),
        (x,),
        [whole(x.shape)],
        jax.ShapeDtypeStruct((count,) + x.shape[1:], x.dtype),
        pl.BlockSpec(block, lambda i, *_: (i,) + zeros),
    )


def order_body(count, place_ref, *refs):
    out = refs[count]
    for s in range(count):
        out[place_ref[s]] = refs[s][...]


def put_in_order(places, pieces):
    count = len(pieces)
    shape = pieces[0].shape
    return call(
        partial(order_body, count),
        (1,),
        (places,),
        pieces,
        [whole(shape)] * count,
        jax.ShapeDtypeStruct((count,) + shape, pieces[0].dtype),
        whole((count,) + shape),
    )


def extend_body(rows, place_ref, kv_ref, left_ref, right_ref, *refs):
    out = refs[NGLOB]
    out[0] = left_ref[...]
    for r in range(rows):
        out[1 + r] = kv_ref[r]
    out[rows + 1] = right_ref[...]
    for s in range(NGLOB):
        out[rows + 2 + place_ref[s]] = refs[s][...]


def extend(places, kv_rows, left, right, summary):
    rows = kv_rows.shape[0]
    shape = left.shape
    full = (rows + 2 + NGLOB,) + shape
    return call(
        partial(extend_body, rows),
        (1,),
        (places,),
        (kv_rows, left, right, *summary),
        [whole(kv_rows.shape)] + [whole(shape)] * (2 + NGLOB),
        jax.ShapeDtypeStruct(full, kv_rows.dtype),
        whole(full),
    )


def local_scores(slot_ref, edge_ref, row, rows, kv_ref, q, h):
    cols = slice(h * HEAD_DIM, (h + 1) * HEAD_DIM)
    parts = []
    for j in range(SLOTS):
        s = dot_nt(kv_ref[slot_ref[row * SLOTS + j], 0, :, cols], q) * SCALE
        if j == 0:
            s = jnp.where((row == 0) & (edge_ref[0] != 0), -jnp.inf, s)
        if j == 2:
            s = jnp.where((row == rows - 1) & (edge_ref[1] != 0), -jnp.inf, s)
        parts.append(s)
    return parts


def local_stats_body(rows, heads, slot_ref, edge_ref, x_ref, kv_ref, o_ref):
    row = pl.program_id(0)
    for h in range(heads):
        cols = slice(h * HEAD_DIM, (h + 1) * HEAD_DIM)
        q = x_ref[0, 0, :, cols]
        g = x_ref[0, 1, :, cols]
        scores = local_scores(slot_ref, edge_ref, row, rows, kv_ref, q, h)
        top = jnp.max(scores[0], axis=0, keepdims=True)
        for s in scores[1:]:
            top = jnp.maximum(top, jnp.max(s, axis=0, keepdims=True))
        total = jnp.zeros_like(top)
        mean = jnp.zeros_like(top)
        for j in range(SLOTS):
            p = jnp.exp(scores[j] - top)
            dp = dot_nt(kv_ref[slot_ref[row * SLOTS + j], 1, :, cols], g)
            total += jnp.sum(p, axis=0, keepdims=True)
            mean += jnp.sum(p * dp, axis=0, keepdims=True)
        o_ref[0, h : h + 1, :] = top + jnp.log(total)
        o_ref[0, heads + h : heads + h + 1, :] = mean / total


def entry_stats_body(heads, own_ref, valid_ref, x_ref, kv_ref, o_ref):
    e = pl.program_id(0)
    own = own_ref[e] + 1

    @pl.when(valid_ref[e] != 0)
    def _():
        for h in range(heads):
            cols = slice(h * HEAD_DIM, (h + 1) * HEAD_DIM)
            s = dot_nt(kv_ref[own, 0, :, cols], x_ref[0, 0, :, cols]) * SCALE
            dp = dot_nt(kv_ref[own, 1, :, cols], x_ref[0, 1, :, cols])
            top = jnp.max(s, axis=0, keepdims=True)
            p = jnp.exp(s - top)
            total = jnp.sum(p, axis=0, keepdims=True)
            o_ref[0, h : h + 1, :] = top + jnp.log(total)
            o_ref[0, heads + h : heads + h + 1, :] = jnp.sum(p * dp, axis=0, keepdims=True) / total

    @pl.when(valid_ref[e] == 0)
    def _():
        o_ref[...] = jnp.zeros_like(o_ref)


def place_of(e, nz):
    return (e % NX) * nz + e // NX


def combine_body(rows, heads, count, nz, owner_ref, row_ref, loc_ref, rem_ref, ld_ref, out_ref):
    for r in range(rows):
        parts = [loc_ref[r]]
        for j in range(RAND):
            o = owner_ref[r * RAND + j]
            parts.append(rem_ref[place_of(o, nz)])
        logs = [p[:heads] for p in parts]
        means = [p[heads:] for p in parts]
        top = jnp.maximum(jnp.maximum(logs[0], logs[1]), jnp.maximum(logs[2], logs[3]))
        weights = [jnp.exp(x - top) for x in logs]
        total = sum(weights[1:], weights[0])
        mean = sum([w * m for w, m in zip(weights[1:], means[1:])], weights[0] * means[0])
        ld_ref[r, :heads] = top + jnp.log(total)
        ld_ref[r, heads:] = mean / total
    for o in range(count):
        out_ref[place_of(o, nz)] = ld_ref[row_ref[o]]


def entry_grads_body(
    heads, own_ref, valid_ref, x_ref, ld_ref, kv_ref, dq_ref, acc_ref
):
    e = pl.program_id(0)
    own = own_ref[e]

    @pl.when(e == 0)
    def _():
        acc_ref[...] = jnp.zeros_like(acc_ref)

    @pl.when(valid_ref[e] != 0)
    def _():
        for h in range(heads):
            cols = slice(h * HEAD_DIM, (h + 1) * HEAD_DIM)
            q = x_ref[0, 0, :, cols]
            g = x_ref[0, 1, :, cols]
            k = kv_ref[own + 1, 0, :, cols]
            v = kv_ref[own + 1, 1, :, cols]
            p = jnp.exp(dot_nt(k, q) * SCALE - ld_ref[0, h : h + 1, :])
            dp = dot_nt(v, g)
            ds = (p * (dp - ld_ref[0, heads + h : heads + h + 1, :])).astype(BF16)
            acc_ref[own, 0, :, cols] += dot_nn(ds, q)
            acc_ref[own, 1, :, cols] += dot_nn(p.astype(BF16), g)
            dq_ref[0, :, cols] = (dot_tn(ds, k) * SCALE).astype(BF16)

    @pl.when(valid_ref[e] == 0)
    def _():
        dq_ref[...] = jnp.zeros_like(dq_ref)


def local_grads_body(
    rows, heads, slot_ref, edge_ref, x_ref, ld_ref, kv_ref, dq_ref, rows_ref, side_ref, acc_ref
):
    row = pl.program_id(0)

    @pl.when(row == 0)
    def _():
        acc_ref[...] = jnp.zeros_like(acc_ref)

    for h in range(heads):
        cols = slice(h * HEAD_DIM, (h + 1) * HEAD_DIM)
        q = x_ref[0, 0, :, cols]
        g = x_ref[0, 1, :, cols]
        log = ld_ref[0, h : h + 1, :]
        mean = ld_ref[0, heads + h : heads + h + 1, :]
        scores = local_scores(slot_ref, edge_ref, row, rows, kv_ref, q, h)
        dq = jnp.zeros((BLOCK, HEAD_DIM), F32)
        for j in range(SLOTS):
            slot = slot_ref[row * SLOTS + j]
            p = jnp.exp(scores[j] - log)
            dp = dot_nt(kv_ref[slot, 1, :, cols], g)
            ds = (p * (dp - mean)).astype(BF16)
            acc_ref[slot, 0, :, cols] += dot_nn(ds, q)
            acc_ref[slot, 1, :, cols] += dot_nn(p.astype(BF16), g)
            dq += dot_tn(ds, kv_ref[slot, 0, :, cols])
        dq_ref[0, :, cols] = dq * SCALE

    @pl.when(row == rows - 1)
    def _():
        sources = [0, rows + 1] + [rows + 2 + s for s in range(NGLOB)]
        for place, source in enumerate(sources):
            side_ref[place, 0] = (acc_ref[source, 0] * SCALE).astype(BF16)
            side_ref[place, 1] = acc_ref[source, 1].astype(BF16)
        for r in range(rows):
            rows_ref[r] = acc_ref[1 + r]


def finish_kv_body(
    rows, first_ref, loc_ref, rand_ref, left_ref, right_ref, s0_ref, s1_ref, s2_ref, s3_ref, o_ref
):
    row = pl.program_id(0)
    both = loc_ref[0] + rand_ref[0]
    o = [both[0] * SCALE, both[1]]
    at_first = (row == 0).astype(F32)
    at_last = (row == rows - 1).astype(F32)
    for t in range(2):
        total = o[t] + at_first * left_ref[t].astype(F32) + at_last * right_ref[t].astype(F32)
        for g, s_ref in enumerate((s0_ref, s1_ref, s2_ref, s3_ref)):
            here = ((row == g) & (first_ref[0] != 0)).astype(F32)
            total += here * s_ref[t].astype(F32)
        o_ref[0, t] = total.astype(BF16)


def finish_q_body(owner_ref, loc_ref, a_ref, b_ref, c_ref, o_ref):
    o_ref[0] = (
        loc_ref[0] + a_ref[0].astype(F32) + b_ref[0].astype(F32) + c_ref[0].astype(F32)
    ).astype(BF16)


def exchange_small(x):
    nz = lax.axis_size("z")
    x = x.reshape((NX, nz) + x.shape[1:])
    x = lax.all_to_all(x, "x", split_axis=0, concat_axis=0, tiled=True)
    x = lax.all_to_all(x, "z", split_axis=1, concat_axis=1, tiled=True)
    return x.reshape((NX * nz,) + x.shape[2:])


def ring(axis, shift):
    count = lax.axis_size(axis)
    return [(i, (i + shift) % count) for i in range(count)]


def on_device(query, keys, values, grad_out, random_owner, random_within, global_ids):
    nz = lax.axis_size("z")
    nh = lax.axis_size("head")
    zi = lax.axis_index("z")
    xi = lax.axis_index("x")
    hi = lax.axis_index("head")
    count = nz * NX
    ctx_index = zi * NX + xi
    tokens, width = query.shape
    features = width // nh
    heads = features // HEAD_DIM
    rows = nh
    unit = (2, BLOCK, features)
    stat = (2 * heads, BLOCK)

    entries = rows * RAND
    owner_all = random_owner.reshape(count, entries)
    within_all = random_within.reshape(count, entries)
    hit = owner_all == ctx_index
    own = jnp.sum(jnp.where(hit, within_all, 0), axis=1).astype(jnp.int32)
    valid = jnp.any(hit, axis=1).astype(jnp.int32)
    owner_mine = lax.dynamic_index_in_dim(owner_all, ctx_index, 0, keepdims=False)
    named = owner_mine[:, None] == jnp.arange(count, dtype=jnp.int32)[None, :]
    entry_row = (jnp.arange(entries, dtype=jnp.int32) // RAND)[:, None]
    row_of = jnp.sum(jnp.where(named, entry_row, 0), axis=0).astype(jnp.int32)
    global_mine = lax.dynamic_slice_in_dim(global_ids, ctx_index * rows, rows, 0)
    row_ids = jnp.arange(rows, dtype=jnp.int32)[:, None]
    slots = jnp.concatenate(
        [row_ids, row_ids + 1, row_ids + 2, global_mine + rows + 2], axis=1
    ).reshape(-1)
    edges = jnp.stack([ctx_index == 0, ctx_index == count - 1]).astype(jnp.int32)

    def split(a, b):
        a = a.reshape(BLOCK, nh, features).transpose(1, 0, 2)
        b = b.reshape(BLOCK, nh, features).transpose(1, 0, 2)
        return jnp.stack([a, b], 1)

    x_rows = lax.all_to_all(split(query, grad_out), "head", split_axis=0, concat_axis=0, tiled=True)
    x_sent = pick_rows(row_of, x_rows, count)
    x_in = lax.all_to_all(x_sent, CTX, split_axis=0, concat_axis=0, tiled=True)

    kv_split = split(keys, values)
    pieces = []
    for s in range(nh):
        piece = lax.dynamic_index_in_dim(kv_split, (hi + s) % nh, 0, keepdims=False)
        pieces.append(piece if s == 0 else lax.ppermute(piece, "head", ring("head", s)))
    places = (hi - jnp.arange(nh, dtype=jnp.int32)) % nh
    kv_rows = put_in_order(places, pieces)
    left = lax.ppermute(kv_rows[rows - 1], CTX, [(i, (i + 1) % count) for i in range(count)])
    right = lax.ppermute(kv_rows[0], CTX, [((i + 1) % count, i) for i in range(count)])
    summary = kv_rows[0]
    for g in range(1, NGLOB):
        came = lax.ppermute(kv_rows[g], CTX, [(0, g)])
        summary = jnp.where(xi == g, came, summary)
    step = nz // 2
    while step:
        pairs = [(z, z + step) for z in range(0, nz, 2 * step)]
        came = lax.ppermute(summary, "z", pairs)
        summary = jnp.where(zi % (2 * step) == step, came, summary)
        step //= 2
    summaries = [summary] + [lax.ppermute(summary, "x", ring("x", s)) for s in range(1, NX)]
    sum_places = (xi - jnp.arange(NX, dtype=jnp.int32)) % NX
    kv_all = extend(sum_places, kv_rows, left, right, summaries)

    row_spec = pl.BlockSpec((1,) + unit, lambda i, *_: (i, 0, 0, 0))
    stat_spec = pl.BlockSpec((1,) + stat, lambda i, *_: (i, 0, 0))
    placed_spec = pl.BlockSpec((1,) + stat, lambda i, *_: (place_of(i, nz), 0, 0))
    half_spec = pl.BlockSpec((1, BLOCK, features), lambda i, *_: (i, 0, 0))
    shape = jax.ShapeDtypeStruct

    stats_loc = call(
        partial(local_stats_body, rows, heads),
        (rows,),
        (slots, edges),
        (x_rows, kv_all),
        [row_spec, whole(kv_all.shape)],
        shape((rows,) + stat, F32),
        stat_spec,
    )
    stats_out = call(
        partial(entry_stats_body, heads),
        (count,),
        (own, valid),
        (x_in, kv_all),
        [row_spec, whole(kv_all.shape)],
        shape((count,) + stat, F32),
        placed_spec,
    )
    stats_in = exchange_small(stats_out)
    ld, ld_out = call(
        partial(combine_body, rows, heads, count, nz),
        (1,),
        (owner_mine, row_of),
        (stats_loc, stats_in),
        [whole(stats_loc.shape), whole(stats_in.shape)],
        (shape((rows,) + stat, F32), shape((count,) + stat, F32)),
        (whole((rows,) + stat), whole((count,) + stat)),
    )
    ld_in = exchange_small(ld_out)
    dq_out, rand_acc = call(
        partial(entry_grads_body, heads),
        (count,),
        (own, valid),
        (x_in, ld_in, kv_all),
        [row_spec, placed_spec, whole(kv_all.shape)],
        (shape((count, BLOCK, features), BF16), shape((rows,) + unit, F32)),
        (half_spec, whole((rows,) + unit)),
    )
    dq_in = lax.all_to_all(dq_out, CTX, split_axis=0, concat_axis=0, tiled=True)

    side_count = 2 + NGLOB
    dq_loc, loc_acc, side = call(
        partial(local_grads_body, rows, heads),
        (rows,),
        (slots, edges),
        (x_rows, ld, kv_all),
        [row_spec, stat_spec, whole(kv_all.shape)],
        (
            shape((rows, BLOCK, features), F32),
            shape((rows,) + unit, F32),
            shape((side_count,) + unit, BF16),
        ),
        (half_spec, whole((rows,) + unit), whole((side_count,) + unit)),
        [pltpu.VMEM(kv_all.shape, F32)],
    )
    from_left = lax.ppermute(side[1], CTX, [(i, (i + 1) % count) for i in range(count)])
    from_right = lax.ppermute(side[0], CTX, [((i + 1) % count, i) for i in range(count)])
    summed = lax.dynamic_index_in_dim(side, 2 + xi, 0, keepdims=False).astype(F32)
    for s in range(1, NX):
        sent = lax.dynamic_index_in_dim(side, 2 + (xi + s) % NX, 0, keepdims=False)
        summed = summed + lax.ppermute(sent, "x", ring("x", s)).astype(F32)
    step = 1
    while step < nz:
        pairs = [(z + step, z) for z in range(0, nz, 2 * step)]
        summed = summed + lax.ppermute(summed, "z", pairs)
        step *= 2
    total = summed.astype(BF16)
    totals = [total] + [lax.ppermute(total, CTX, [(g, 0)]) for g in range(1, NGLOB)]

    kv_back = call(
        partial(finish_kv_body, rows),
        (rows,),
        (edges,),
        (loc_acc, rand_acc, from_left, from_right, *totals),
        [row_spec, row_spec] + [whole(unit)] * (2 + NGLOB),
        shape((rows,) + unit, BF16),
        row_spec,
    )
    kv_done = lax.all_to_all(kv_back, "head", split_axis=0, concat_axis=0, tiled=True)

    def random_spec(j):
        return pl.BlockSpec((1, BLOCK, features), lambda i, t: (t[i * RAND + j], 0, 0))

    q_back = call(
        finish_q_body,
        (rows,),
        (owner_mine,),
        (dq_loc, dq_in, dq_in, dq_in),
        [half_spec] + [random_spec(j) for j in range(RAND)],
        shape((rows, BLOCK, features), BF16),
        half_spec,
    )
    q_done = lax.all_to_all(q_back, "head", split_axis=0, concat_axis=0, tiled=True)

    def joined(a):
        return a.transpose(1, 0, 2).reshape(tokens, width)

    return joined(q_done), joined(kv_done[:, 0]), joined(kv_done[:, 1])


def solution(mesh):
    count, nh = mesh.devices.shape
    fine = Mesh(mesh.devices.reshape(count // NX, NX, nh), ("z", "x", "head"))
    tokens = P(("z", "x", "head"), None)
    return jax.shard_map(
        on_device,
        mesh=fine,
        in_specs=(tokens,) * 4 + (P(),) * 3,
        out_specs=(tokens,) * 3,
        check_vma=False,
    )
```

time: 884 us -> 630 us (0.71)
  the two profiles are of different devices: /device:TPU:102 before, /device:TPU:1 now
where the time goes in v1:
time: 630 us; the launch traced here: 627 us
  waiting for transfers between devices  329 us (52%)
  Pallas kernels  144 us (23%)
  starting transfers between devices  97.7 us (16%)
  local copies, waits for them, and re-layouts  23.8 us (4%)
  blocking collectives  22.5 us (4%)
  other arithmetic  8.55 us (1%)
    pallas_call x10, Pallas kernels, call(): pl.pallas_call(body, grid_spec=pltpu.PrefetchScalarGridSpec(num_scalar_pr...  144 us
    ppermute x3, waiting for transfers between devices, on_device(): came = lax.ppermute(summary, 'z', pairs)  130 us
    ppermute x3, waiting for transfers between devices, on_device(): summed = summed + lax.ppermute(summed, 'z', pairs)  72.6 us
    all_to_all x1, waiting for transfers between devices, on_device(): lax.all_to_all(split(query, grad_out), 'head', split_axis=0, concat_axis=...  25.5 us
    ppermute x3, waiting for transfers between devices, on_device(): came = lax.ppermute(kv_rows[g], CTX, [(0, g)])  20.7 us
    all_to_all x1, waiting for transfers between devices, on_device(): lax.all_to_all(kv_back, 'head', split_axis=0, concat_axis=0, tiled=True)  19.5 us
    ppermute x7, waiting for transfers between devices, on_device(): lax.ppermute(piece, 'head', ring('head', s))  16.7 us
    all_to_all x1, blocking collectives, exchange_small(): x = lax.all_to_all(x, 'z', split_axis=1, concat_axis=1, tiled=True)  14.4 us
  transfers between devices with their start and end apart: 36, of which 20 were waited for; matrix products, arithmetic and copies ran while one was open for 3% of the time, Pallas kernels for 11%

profile of v1, /device:TPU:1, one launch (start us, length us, event | category | flops | bytes accessed | tf_op | source)
XLA Modules:
  0.0 627.4 jit_solution(10234698263192369167)
XLA Ops:
  0.6 1.7 copy.65
  4.1 1.5 pad_maximum_fusion
  5.6 6.9 %all-to-all-start = ((bf16[8,2,128,512]{3,2,1,0:T(8,128)(2,1)}), bf16[8,2,128,512]{3,2,1,0:T(8,128)(2,1)S(1)}, u32[]{:S(2)}, u32[]{:S(2)}) async-start(bf16[8,2,128,512]{3,2,1,0:T(8,128)(2,1)} %pad_maximum_fusion), calls=%async_computation | async-start | bytes 4194304 | tf_op jit(solution)/shard_map/all_to_all | solution.py:338
  13.4 25.5 %all-to-all-done.x_ref = bf16[8,2,128,512]{3,2,1,0:T(8,128)(2,1)S(1)} async-done(((bf16[8,2,128,512]{3,2,1,0:T(8,128)(2,1)}), bf16[8,2,128,512]{3,2,1,0:T(8,128)(2,1)S(1)}, u32[]{:S(2)}, u32[]{:S(2)}) %all-to-all-start) | async-done | bytes 2097184 | tf_op jit(solution)/shard_map/all_to_all | solution.py:338
  38.9 1.4 copy-done
  40.2 14.0 %shard_map.97 = bf16[32,2,128,512]{3,2,1,0:T(8,128)(2,1)} custom-call(s32[32]{0:T(128)} %select_reduce_fusion.row_ref, bf16[8,2,128,512]{3,2,1,0:T(8,128)(2,1)} %copy-done), custom_call_target="tpu_custom_call" | custom-call | tf_op jit(solution)/shard_map/pallas_call | solution.py:45
  54.2 10.5 %all-to-all-start.1 = ((bf16[32,2,128,512]{3,2,1,0:T(8,128)(2,1)}), bf16[32,2,128,512]{3,2,1,0:T(8,128)(2,1)}, u32[]{:S(2)}, u32[]{:S(2)}) async-start(bf16[32,2,128,512]{3,2,1,0:T(8,128)(2,1)} %shard_map.97), calls=%async_computation.1 | async-start | bytes 16777216 | tf_op jit(solution)/shard_map/all_to_all | solution.py:340
  64.8 1.4 bitcast_bitcast_fusion
  69.7 1.3 collective-permute-start
  71.0 1.7 collective-permute-start.1
  73.1 3.8 collective-permute-start.2
  77.0 3.2 collective-permute-done.4.refs_5_
  81.9 4.0 collective-permute-done.6.refs_7_
  86.0 8.8 %collective-permute-done.2.refs_3_ = bf16[2,128,512]{2,1,0:T(8,128)(2,1)S(1)} collective-permute-done((bf16[2,128,512]{2,1,0:T(8,128)(2,1)S(1)}, bf16[2,128,512]{2,1,0:T(8,128)(2,1)S(1)}, u32[]{:S(2)}, u32[]{:S(2)}) %collective-permute-start.2) | collective-permute-done | bytes 262176 | tf_op jit(solution)/shard_map/ppermute | solution.py:346
  95.7 3.7 shard_map.94.kv_ref
  99.4 1.4 slice_bitcast_fusion.2
  100.8 3.4 collective-permute-start.11
  104.1 2.2 collective-permute-start.10
  106.3 1.3 collective-permute-start.9
  107.6 8.8 %collective-permute-done.11 = bf16[2,128,512]{2,1,0:T(8,128)(2,1)S(1)} collective-permute-done((bf16[2,128,512]{2,1,0:T(8,128)(2,1)S(1)}, bf16[2,128,512]{2,1,0:T(8,128)(2,1)S(1)}, u32[]{:S(2)}, u32[]{:S(2)}) %collective-permute-start.11) | collective-permute-done | bytes 262176 | tf_op jit(solution)/shard_map/ppermute | solution.py:353
  116.4 11.9 %collective-permute-done.10 = bf16[2,128,512]{2,1,0:T(8,128)(2,1)S(1)} collective-permute-done((bf16[2,128,512]{2,1,0:T(8,128)(2,1)S(1)}, bf16[2,128,512]{2,1,0:T(8,128)(2,1)S(1)}, u32[]{:S(2)}, u32[]{:S(2)}) %collective-permute-start.10) | collective-permute-done | bytes 262176 | tf_op jit(solution)/shard_map/ppermute | solution.py:353
  129.3 1.3 collective-permute-start.12
  130.6 123.3 %collective-permute-done.12 = bf16[2,128,512]{2,1,0:T(8,128)(2,1)S(1)} collective-permute-done((bf16[2,128,512]{2,1,0:T(8,128)(2,1)S(1)}, bf16[2,128,512]{2,1,0:T(8,128)(2,1)S(1)}, u32[]{:S(2)}, u32[]{:S(2)}) %collective-permute-start.12) | collective-permute-done | bytes 262176 | tf_op jit(solution)/shard_map/ppermute | solution.py:358
  254.0 1.3 collective-permute-start.13
  255.3 4.1 collective-permute-done.13
  259.4 1.3 collective-permute-start.14
  260.8 1.5 collective-permute-start.7
  262.3 2.1 collective-permute-done.14
  264.5 5.3 collective-permute-start.17
  272.6 10.8 %collective-permute-done.17.refs_3_ = bf16[2,128,512]{2,1,0:T(8,128)(2,1)S(1)} collective-permute-done((bf16[2,128,512]{2,1,0:T(8,128)(2,1)S(1)}, bf16[2,128,512]{2,1,0:T(8,128)(2,1)S(1)}, u32[]{:S(2)}, u32[]{:S(2)}) %collective-permute-start.17) | collective-permute-done | bytes 262176 | tf_op jit(solution)/shard_map/ppermute | solution.py:361
  284.9 4.7 shard_map.95.kv_ref
  289.6 23.8 %shard_map.98 = f32[32,8,128]{2,1,0:T(8,128)} custom-call(s32[32]{0:T(128)} %reduce_sum.28.own_ref, s32[32]{0:T(128)} %convert_element_type.25.valid_ref, bf16[32,2,128,512]{3,2,1,0:T(8,128)(2,1)} %all-to-all-done.1.x_ref, bf16[14,2,128,512]{3,2,1,0:T(8,128)(2,1)} %shard_map.95.kv_ref), custom_call_target="tpu_custom_call" | custom-call | tf_op jit(solution)/shard_map/pallas_call | solution.py:45
  313.4 4.8 all-to-all-start.2
  318.2 4.8 all-to-all-done.2
  323.7 11.8 %all-to-all-start.3 = ((f32[4,8,8,128]{3,2,0,1:T(8,128)}), f32[4,8,8,128]{3,2,0,1:T(8,128)S(1)}, u32[]{:S(2)}, u32[]{:S(2)}) async-start(f32[4,8,8,128]{3,2,0,1:T(8,128)} %copy.71), calls=%async_computation.3 | async-start | bytes 262144 | tf_op jit(solution)/shard_map/all_to_all | solution.py:292
  336.8 12.2 %shard_map.96.loc_ref = f32[8,8,128]{2,1,0:T(8,128)} custom-call(s32[40]{0:T(128)} %reshape.82.slot_ref, s32[2]{0:T(128)} %add_convert_fusion.1.edge_ref.first_ref, bf16[8,2,128,512]{3,2,1,0:T(8,128)(2,1)} %copy-done, bf16[14,2,128,512]{3,2,1,0:T(8,128)(2,1)} %shard_map.95.kv_ref), custom_call_target="tpu_custom_call" | custom-call | tf_op jit(solution)/shard_map/pallas_call | solution.py:45
  349.7 2.4 shard_map.99
  352.2 8.1 %all_to_all.45 = f32[4,8,8,128]{3,2,1,0:T(8,128)S(1)} all-to-all(f32[4,8,8,128]{3,2,1,0:T(8,128)} %bitcast.96), channel_id=1, replica_groups=mesh['z'=8,'x'=4,'head'=8] {'x'}, dimensions={0} | all-to-all | bytes 262144 | tf_op jit(solution)/shard_map/all_to_all | solution.py:291
  360.3 14.4 %all_to_all.46 = f32[4,8,8,128]{3,2,0,1:T(8,128)S(1)} all-to-all(f32[4,8,8,128]{3,2,0,1:T(8,128)S(1)} %copy.73), channel_id=1, replica_groups=mesh['z'=8,'x'=4,'head'=8] {'z'}, dimensions={1} | all-to-all | bytes 262144 | tf_op jit(solution)/shard_map/all_to_all | solution.py:292
  375.3 36.2 %shard_map.101 = (bf16[32,128,512]{2,1,0:T(8,128)(2,1)}, f32[8,2,128,512]{3,2,1,0:T(8,128)}) custom-call(s32[32]{0:T(128)} %reduce_sum.28.own_ref, s32[32]{0:T(128)} %convert_element_type.25.valid_ref, bf16[32,2,128,512]{3,2,1,0:T(8,128)(2,1)} %all-to-all-done.1.x_ref, f32[32,8,128]{2,1,0:T(8,128)} %bitcast.94, bf16[14,2,128,512]{3,2,1,0:T(8,128)(2,1)} %shard_map.95.kv_ref), custom_call_target="tpu_custom_call" | custom-call | tf_op jit(solution)/shard_map/pallas_call | solution.py:45
  411.5 5.7 all-to-all-start.6
  417.3 31.2 %shard_map.100 = (f32[8,128,512]{2,1,0:T(8,128)}, f32[8,2,128,512]{3,2,1,0:T(8,128)}, bf16[6,2,128,512]{3,2,1,0:T(8,128)(2,1)}) custom-call(s32[40]{0:T(128)} %reshape.82.slot_ref, s32[2]{0:T(128)} %add_convert_fusion.1.edge_ref.first_ref, bf16[8,2,128,512]{3,2,1,0:T(8,128)(2,1)} %copy-done, f32[8,8,128]{2,1,0:T(8,128)} %get-tuple-element.10.ld_ref, ...), custom_call_target="tpu_custom_call" | custom-call | tf_op jit(solution)/shard_map/pallas_call | solution.py:45
  448.5 1.4 dynamic-slice_bitcast_fusion.2
  451.1 1.5 collective-permute-start.22
  452.7 1.5 collective-permute-start.21
  454.1 9.4 %collective-permute-done.20 = bf16[2,128,512]{2,1,0:T(8,128)(2,1)S(1)} collective-permute-done((bf16[2,128,512]{2,1,0:T(8,128)(2,1)S(1)}, bf16[2,128,512]{2,1,0:T(8,128)(2,1)S(1)}, u32[]{:S(2)}, u32[]{:S(2)}) %collective-permute-start.20) | collective-permute-done | bytes 262176 | tf_op jit(solution)/shard_map/ppermute | solution.py:431
  464.6 1.3 collective-permute-start.23
  465.9 51.0 %collective-permute-done.23 = f32[2,128,512]{2,1,0:T(8,128)S(1)} collective-permute-done((f32[2,128,512]{2,1,0:T(8,128)S(1)}, f32[2,128,512]{2,1,0:T(8,128)S(1)}, u32[]{:S(2)}, u32[]{:S(2)}) %collective-permute-start.23) | collective-permute-done | bytes 524320 | tf_op jit(solution)/shard_map/ppermute | solution.py:435
  517.1 1.3 collective-permute-start.24
  518.4 10.6 %collective-permute-done.24 = f32[2,128,512]{2,1,0:T(8,128)S(1)} collective-permute-done((f32[2,128,512]{2,1,0:T(8,128)S(1)}, f32[2,128,512]{2,1,0:T(8,128)S(1)}, u32[]{:S(2)}, u32[]{:S(2)}) %collective-permute-start.24) | collective-permute-done | bytes 524320 | tf_op jit(solution)/shard_map/ppermute | solution.py:435
  530.4 1.5 collective-permute-start.18
  531.9 11.0 %collective-permute-done.25 = f32[2,128,512]{2,1,0:T(8,128)S(1)} collective-permute-done((f32[2,128,512]{2,1,0:T(8,128)S(1)}, f32[2,128,512]{2,1,0:T(8,128)S(1)}, u32[]{:S(2)}, u32[]{:S(2)}) %collective-permute-start.25) | collective-permute-done | bytes 524320 | tf_op jit(solution)/shard_map/ppermute | solution.py:435
  546.9 11.3 %collective-permute-done.28.s3_ref = bf16[2,128,512]{2,1,0:T(8,128)(2,1)S(1)} collective-permute-done((bf16[2,128,512]{2,1,0:T(8,128)(2,1)S(1)}, bf16[2,128,512]{2,1,0:T(8,128)(2,1)S(1)}, u32[]{:S(2)}, u32[]{:S(2)}) %collective-permute-start.28) | collective-permute-done | bytes 262176 | tf_op jit(solution)/shard_map/ppermute | solution.py:438
  559.1 9.2 %shard_map.103 = bf16[8,2,128,512]{3,2,1,0:T(8,128)(2,1)} custom-call(s32[2]{0:T(128)} %add_convert_fusion.1.edge_ref.first_ref, f32[8,2,128,512]{3,2,1,0:T(8,128)} %get-tuple-element.14.loc_ref, f32[8,2,128,512]{3,2,1,0:T(8,128)} %get-tuple-element.15.rand_ref, bf16[2,128,512]{2,1,0:T(8,128)(2,1)} %copy-done.12, bf16[2,128,512]{2,1,0:T(8,128)(2,1)} %copy-done.11, ...), custom_call_target="tpu_custom_call" | custom-call | tf_op jit(solution)/shard_map/pallas_call | solution.py:45
  568.3 11.4 %all-to-all-start.8 = ((bf16[8,2,128,512]{3,2,1,0:T(8,128)(2,1)}), bf16[8,2,128,512]{3,2,1,0:T(8,128)(2,1)S(1)}, u32[]{:S(2)}, u32[]{:S(2)}) async-start(bf16[8,2,128,512]{3,2,1,0:T(8,128)(2,1)} %shard_map.103), calls=%async_computation.8 | async-start | bytes 4194304 | tf_op jit(solution)/shard_map/all_to_all | solution.py:449
  579.6 6.8 %shard_map.102 = bf16[8,128,512]{2,1,0:T(8,128)(2,1)} custom-call(s32[24]{0:T(128)} %copy-done.25, f32[8,128,512]{2,1,0:T(8,128)} %get-tuple-element.11.loc_ref, bf16[32,128,512]{2,1,0:T(8,128)(2,1)} %all-to-all-done.6.a_ref.b_ref.c_ref, bf16[32,128,512]{2,1,0:T(8,128)(2,1)} %all-to-all-done.6.a_ref.b_ref.c_ref, ...), custom_call_target="tpu_custom_call" | custom-call | tf_op jit(solution)/shard_map/pallas_call | solution.py:45
  586.5 19.5 %all-to-all-done.8 = bf16[8,2,128,512]{3,2,1,0:T(8,128)(2,1)S(1)} async-done(((bf16[8,2,128,512]{3,2,1,0:T(8,128)(2,1)}), bf16[8,2,128,512]{3,2,1,0:T(8,128)(2,1)S(1)}, u32[]{:S(2)}, u32[]{:S(2)}) %all-to-all-start.8) | async-done | bytes 2097184 | tf_op jit(solution)/shard_map/all_to_all | solution.py:449
  606.0 4.3 all-to-all-start.7
  610.3 1.5 slice_bitcast_fusion
  611.9 1.7 copy.77
  613.6 1.3 copy.80
  615.5 1.3 copy.79
  616.9 8.6 %all-to-all-done.7 = bf16[8,128,512]{2,1,0:T(8,128)(2,1)S(1)} async-done(((bf16[8,128,512]{2,1,0:T(8,128)(2,1)}), bf16[8,128,512]{2,1,0:T(8,128)(2,1)S(1)}, u32[]{:S(2)}, u32[]{:S(2)}) %all-to-all-start.7) | async-done | bytes 1048608 | tf_op jit(solution)/shard_map/all_to_all | solution.py:463
  626.1 1.3 copy.78
  (124 shorter events, 28.0 us)
Async XLA Ops:
  0.6 2.3 copy-start.3
  5.6 6.9 %copy-start.23 = (s32[256,3]{0,1:T(4,128)S(1)}, s32[256,3]{0,1:T(4,128)}, u32[]{:S(2)}) copy-start(s32[256,3]{0,1:T(4,128)} %param.11) | copy-start | bytes 9220
  5.6 33.2 %all-to-all-start = ((bf16[8,2,128,512]{3,2,1,0:T(8,128)(2,1)}), bf16[8,2,128,512]{3,2,1,0:T(8,128)(2,1)S(1)}, u32[]{:S(2)}, u32[]{:S(2)}) async-start(bf16[8,2,128,512]{3,2,1,0:T(8,128)(2,1)} %pad_maximum_fusion), calls=%async_computation | async-start | bytes 4194304 | tf_op jit(solution)/shard_map/all_to_all | solution.py:338
  12.8 41.4 %copy-start.25 = (s32[24]{0:T(128)}, s32[24]{0:T(128)S(1)}, u32[]{:S(2)}) copy-start(s32[24]{0:T(128)S(1)} %fusion.21.owner_ref) | copy-start | bytes 292
  38.9 1.4 copy-start
  54.2 10.5 %copy-start.4 = (bf16[128,4096]{1,0:T(8,128)(2,1)S(1)}, bf16[128,4096]{1,0:T(8,128)(2,1)}, u32[]{:S(2)}) copy-start(bf16[128,4096]{1,0:T(8,128)(2,1)} %param.9) | copy-start | bytes 3145732
  54.2 235.3 %all-to-all-start.1 = ((bf16[32,2,128,512]{3,2,1,0:T(8,128)(2,1)}), bf16[32,2,128,512]{3,2,1,0:T(8,128)(2,1)}, u32[]{:S(2)}, u32[]{:S(2)}) async-start(bf16[32,2,128,512]{3,2,1,0:T(8,128)(2,1)} %shard_map.97), calls=%async_computation.1 | async-start | bytes 16777216 | tf_op jit(solution)/shard_map/all_to_all | solution.py:340
  66.3 6.8 %collective-permute-start.5 = (bf16[2,128,512]{2,1,0:T(8,128)(2,1)S(1)}, bf16[2,128,512]{2,1,0:T(8,128)(2,1)S(1)}, u32[]{:S(2)}, u32[]{:S(2)}) collective-permute-start(bf16[2,128,512]{2,1,0:T(8,128)(2,1)S(1)} %get-tuple-element.44), channel_id=1, source_target_pairs={{0,6},{1,7},{2,0},{3,1},{4,2},{5,3},{6,4},{7,5},{8,14},{9,15},{10,... | collective-permute-start | bytes 786440 | tf_op jit(solution)/shard_map/ppermute | solution.py:346
  67.3 12.9 %collective-permute-start.4 = (bf16[2,128,512]{2,1,0:T(8,128)(2,1)S(1)}, bf16[2,128,512]{2,1,0:T(8,128)(2,1)S(1)}, u32[]{:S(2)}, u32[]{:S(2)}) collective-permute-start(bf16[2,128,512]{2,1,0:T(8,128)(2,1)S(1)} %get-tuple-element.45), channel_id=1, source_target_pairs={{0,5},{1,6},{2,7},{3,0},{4,1},{5,2},{6,3},{7,4},{8,13},{9,14},{10,... | collective-permute-start | bytes 786440 | tf_op jit(solution)/shard_map/ppermute | solution.py:346
  69.2 16.6 %collective-permute-start.6 = (bf16[2,128,512]{2,1,0:T(8,128)(2,1)S(1)}, bf16[2,128,512]{2,1,0:T(8,128)(2,1)S(1)}, u32[]{:S(2)}, u32[]{:S(2)}) collective-permute-start(bf16[2,128,512]{2,1,0:T(8,128)(2,1)S(1)} %get-tuple-element.38), channel_id=1, source_target_pairs={{0,7},{1,0},{2,1},{3,2},{4,3},{5,4},{6,5},{7,6},{8,15},{9,8},{10,9... | collective-permute-start | bytes 786440 | tf_op jit(solution)/shard_map/ppermute | solution.py:346
  69.7 16.1 %collective-permute-start = (bf16[2,128,512]{2,1,0:T(8,128)(2,1)S(1)}, bf16[2,128,512]{2,1,0:T(8,128)(2,1)S(1)}, u32[]{:S(2)}, u32[]{:S(2)}) collective-permute-start(bf16[2,128,512]{2,1,0:T(8,128)(2,1)S(1)} %get-tuple-element.40), channel_id=1, source_target_pairs={{0,1},{1,2},{2,3},{3,4},{4,5},{5,6},{6,7},{7,0},{8,9},{9,10},{10,1... | collective-permute-start | bytes 786440 | tf_op jit(solution)/shard_map/ppermute | solution.py:346
  71.0 15.0 %collective-permute-start.1 = (bf16[2,128,512]{2,1,0:T(8,128)(2,1)S(1)}, bf16[2,128,512]{2,1,0:T(8,128)(2,1)S(1)}, u32[]{:S(2)}, u32[]{:S(2)}) collective-permute-start(bf16[2,128,512]{2,1,0:T(8,128)(2,1)S(1)} %get-tuple-element.41), channel_id=1, source_target_pairs={{0,2},{1,3},{2,4},{3,5},{4,6},{5,7},{6,0},{7,1},{8,10},{9,11},{10,... | collective-permute-start | bytes 786440 | tf_op jit(solution)/shard_map/ppermute | solution.py:346
  73.1 21.7 %copy-start.6 = (bf16[2,128,512]{2,1,0:T(8,128)(2,1)}, bf16[2,128,512]{2,1,0:T(8,128)(2,1)S(1)}, u32[]{:S(2)}) copy-start(bf16[2,128,512]{2,1,0:T(8,128)(2,1)S(1)} %collective-permute-done.5.refs_6_) | copy-start | bytes 786436
  73.1 21.7 %collective-permute-start.2 = (bf16[2,128,512]{2,1,0:T(8,128)(2,1)S(1)}, bf16[2,128,512]{2,1,0:T(8,128)(2,1)S(1)}, u32[]{:S(2)}, u32[]{:S(2)}) collective-permute-start(bf16[2,128,512]{2,1,0:T(8,128)(2,1)S(1)} %get-tuple-element.42), channel_id=1, source_target_pairs={{0,3},{1,4},{2,5},{3,6},{4,7},{5,0},{6,1},{7,2},{8,11},{9,12},{10,... | collective-permute-start | bytes 786440 | tf_op jit(solution)/shard_map/ppermute | solution.py:346
  80.2 14.7 %copy-start.7 = (bf16[2,128,512]{2,1,0:T(8,128)(2,1)}, bf16[2,128,512]{2,1,0:T(8,128)(2,1)S(1)}, u32[]{:S(2)}) copy-start(bf16[2,128,512]{2,1,0:T(8,128)(2,1)S(1)} %collective-permute-done.4.refs_5_) | copy-start | bytes 786436
  80.2 14.7 %collective-permute-start.3 = (bf16[2,128,512]{2,1,0:T(8,128)(2,1)S(1)}, bf16[2,128,512]{2,1,0:T(8,128)(2,1)S(1)}, u32[]{:S(2)}, u32[]{:S(2)}) collective-permute-start(bf16[2,128,512]{2,1,0:T(8,128)(2,1)S(1)} %get-tuple-element.43), channel_id=1, source_target_pairs={{0,4},{1,5},{2,6},{3,7},{4,0},{5,1},{6,2},{7,3},{8,12},{9,13},{10,... | collective-permute-start | bytes 786440 | tf_op jit(solution)/shard_map/ppermute | solution.py:346
  85.8 9.1 %copy-start.8 = (bf16[2,128,512]{2,1,0:T(8,128)(2,1)}, bf16[2,128,512]{2,1,0:T(8,128)(2,1)S(1)}, u32[]{:S(2)}) copy-start(bf16[2,128,512]{2,1,0:T(8,128)(2,1)S(1)} %collective-permute-done.6.refs_7_) | copy-start | bytes 786436
  85.8 9.1 %copy-start.9 = (bf16[2,128,512]{2,1,0:T(8,128)(2,1)}, bf16[2,128,512]{2,1,0:T(8,128)(2,1)S(1)}, u32[]{:S(2)}) copy-start(bf16[2,128,512]{2,1,0:T(8,128)(2,1)S(1)} %collective-permute-done.refs_1_) | copy-start | bytes 786436
  86.0 8.9 %copy-start.10 = (bf16[2,128,512]{2,1,0:T(8,128)(2,1)}, bf16[2,128,512]{2,1,0:T(8,128)(2,1)S(1)}, u32[]{:S(2)}) copy-start(bf16[2,128,512]{2,1,0:T(8,128)(2,1)S(1)} %collective-permute-done.1.refs_2_) | copy-start | bytes 786436
  94.9 0.7 copy-start.13
  94.9 0.8 copy-start.15
  100.8 170.5 %copy-start.24 = (s32[256,3]{0,1:T(4,128)S(1)}, s32[256,3]{0,1:T(4,128)}, u32[]{:S(2)}) copy-start(s32[256,3]{0,1:T(4,128)} %param.12) | copy-start | bytes 9220
  100.8 15.6 %collective-permute-start.11 = (bf16[2,128,512]{2,1,0:T(8,128)(2,1)S(1)}, bf16[2,128,512]{2,1,0:T(8,128)(2,1)S(1)}, u32[]{:S(2)}, u32[]{:S(2)}) collective-permute-start(bf16[2,128,512]{2,1,0:T(8,128)(2,1)S(1)} %get-tuple-element.33), channel_id=1, source_target_pairs={{0,8},{1,9},{2,10},{3,11},{4,12},{5,13},{6,14},{7,15}} | collective-permute-start | bytes 786440 | tf_op jit(solution)/shard_map/ppermute | solution.py:353
  104.1 24.2 %collective-permute-start.10 = (bf16[2,128,512]{2,1,0:T(8,128)(2,1)S(1)}, bf16[2,128,512]{2,1,0:T(8,128)(2,1)S(1)}, u32[]{:S(2)}, u32[]{:S(2)}) collective-permute-start(bf16[2,128,512]{2,1,0:T(8,128)(2,1)S(1)} %get-tuple-element.34), channel_id=1, source_target_pairs={{0,16},{1,17},{2,18},{3,19},{4,20},{5,21},{6,22},{7,23}} | collective-permute-start | bytes 786440 | tf_op jit(solution)/shard_map/ppermute | solution.py:353
  106.3 22.0 %collective-permute-start.9 = (bf16[2,128,512]{2,1,0:T(8,128)(2,1)S(1)}, bf16[2,128,512]{2,1,0:T(8,128)(2,1)S(1)}, u32[]{:S(2)}, u32[]{:S(2)}) collective-permute-start(bf16[2,128,512]{2,1,0:T(8,128)(2,1)S(1)} %get-tuple-element.35), channel_id=1, source_target_pairs={{0,24},{1,25},{2,26},{3,27},{4,28},{5,29},{6,30},{7,31}} | collective-permute-start | bytes 786440 | tf_op jit(solution)/shard_map/ppermute | solution.py:353
  129.3 124.6 %collective-permute-start.12 = (bf16[2,128,512]{2,1,0:T(8,128)(2,1)S(1)}, bf16[2,128,512]{2,1,0:T(8,128)(2,1)S(1)}, u32[]{:S(2)}, u32[]{:S(2)}) collective-permute-start(bf16[2,128,512]{2,1,0:T(8,128)(2,1)S(1)} %select_select_fusion), channel_id=1, source_target_pairs={{0,128},{1,129},{2,130},{3,131},{4,132},{5,133},{6,134},{7,135},{8... | collective-permute-start | bytes 786440 | tf_op jit(solution)/shard_map/ppermute | solution.py:358
  254.0 5.4 collective-permute-start.13
  259.4 5.0 collective-permute-start.14
  260.7 11.8 %collective-permute-start.8 = (bf16[2,128,512]{2,1,0:T(8,128)(2,1)S(1)}, bf16[2,128,512]{2,1,0:T(8,128)(2,1)S(1)}, u32[]{:S(2)}, u32[]{:S(2)}) collective-permute-start(bf16[2,128,512]{2,1,0:T(8,128)(2,1)S(1)} %get-tuple-element.36), channel_id=1, source_target_pairs={{8,0},{16,8},{24,16},{32,24},{40,32},{48,40},{56,48},{64,56},{72,6... | collective-permute-start | bytes 786440 | tf_op jit(solution)/shard_map/ppermute | solution.py:350
  260.8 11.7 %collective-permute-start.7 = (bf16[2,128,512]{2,1,0:T(8,128)(2,1)S(1)}, bf16[2,128,512]{2,1,0:T(8,128)(2,1)S(1)}, u32[]{:S(2)}, u32[]{:S(2)}) collective-permute-start(bf16[2,128,512]{2,1,0:T(8,128)(2,1)S(1)} %get-tuple-element.37), channel_id=1, source_target_pairs={{0,8},{8,16},{16,24},{24,32},{32,40},{40,48},{48,56},{56,64},{64,7... | collective-permute-start | bytes 786440 | tf_op jit(solution)/shard_map/ppermute | solution.py:349
  264.5 18.9 %copy-start.5 = (bf16[2,128,512]{2,1,0:T(8,128)(2,1)}, bf16[2,128,512]{2,1,0:T(8,128)(2,1)S(1)}, u32[]{:S(2)}) copy-start(bf16[2,128,512]{2,1,0:T(8,128)(2,1)S(1)} %broadcast_select_fusion.2.refs_0_) | copy-start | bytes 786436
  264.5 18.9 %collective-permute-start.17 = (bf16[2,128,512]{2,1,0:T(8,128)(2,1)S(1)}, bf16[2,128,512]{2,1,0:T(8,128)(2,1)S(1)}, u32[]{:S(2)}, u32[]{:S(2)}) collective-permute-start(bf16[2,128,512]{2,1,0:T(8,128)(2,1)S(1)} %broadcast_select_fusion.2.refs_0_), channel_id=1, source_target_pairs={{0,24},{8,0},{16,8},{24,16},{1,25},{9,1},{17,9},{25,17},{2,26},{10... | collective-permute-start | bytes 786440 | tf_op jit(solution)/shard_map/ppermute | solution.py:361
  269.8 13.6 %collective-permute-start.16 = (bf16[2,128,512]{2,1,0:T(8,128)(2,1)S(1)}, bf16[2,128,512]{2,1,0:T(8,128)(2,1)S(1)}, u32[]{:S(2)}, u32[]{:S(2)}) collective-permute-start(bf16[2,128,512]{2,1,0:T(8,128)(2,1)S(1)} %broadcast_select_fusion.2.refs_0_), channel_id=1, source_target_pairs={{0,16},{8,24},{16,0},{24,8},{1,17},{9,25},{17,1},{25,9},{2,18},{10... | collective-permute-start | bytes 786440 | tf_op jit(solution)/shard_map/ppermute | solution.py:361
  269.8 13.6 %collective-permute-start.15 = (bf16[2,128,512]{2,1,0:T(8,128)(2,1)S(1)}, bf16[2,128,512]{2,1,0:T(8,128)(2,1)S(1)}, u32[]{:S(2)}, u32[]{:S(2)}) collective-permute-start(bf16[2,128,512]{2,1,0:T(8,128)(2,1)S(1)} %broadcast_select_fusion.2.refs_0_), channel_id=1, source_target_pairs={{0,8},{8,16},{16,24},{24,0},{1,9},{9,17},{17,25},{25,1},{2,10},{10... | collective-permute-start | bytes 786440 | tf_op jit(solution)/shard_map/ppermute | solution.py:361
  272.6 10.8 %copy-start.18 = (bf16[2,128,512]{2,1,0:T(8,128)(2,1)}, bf16[2,128,512]{2,1,0:T(8,128)(2,1)S(1)}, u32[]{:S(2)}) copy-start(bf16[2,128,512]{2,1,0:T(8,128)(2,1)S(1)} %collective-permute-done.8.right_ref) | copy-start | bytes 786436
  272.6 10.8 %copy-start.19 = (bf16[2,128,512]{2,1,0:T(8,128)(2,1)}, bf16[2,128,512]{2,1,0:T(8,128)(2,1)S(1)}, u32[]{:S(2)}) copy-start(bf16[2,128,512]{2,1,0:T(8,128)(2,1)S(1)} %collective-permute-done.7.left_ref) | copy-start | bytes 786436
  283.3 0.7 copy-start.20
  283.3 0.8 copy-start.21
  284.2 0.7 copy-start.22
  289.6 45.9 %copy-start.26 = (s32[256,2]{0,1:T(2,128)S(1)}, s32[256,2]{0,1:T(2,128)}, u32[]{:S(2)}) copy-start(s32[256,2]{0,1:T(2,128)} %param.13) | copy-start | bytes 6148
  313.4 9.7 %all-to-all-start.2 = ((f32[4,8,8,128]{3,2,1,0:T(8,128)}), f32[4,8,8,128]{3,2,1,0:T(8,128)S(1)}, u32[]{:S(2)}, u32[]{:S(2)}) async-start(f32[4,8,8,128]{3,2,1,0:T(8,128)} %bitcast.93), calls=%async_computation.2 | async-start | bytes 262144 | tf_op jit(solution)/shard_map/all_to_all | solution.py:291
  323.7 25.4 %all-to-all-start.3 = ((f32[4,8,8,128]{3,2,0,1:T(8,128)}), f32[4,8,8,128]{3,2,0,1:T(8,128)S(1)}, u32[]{:S(2)}, u32[]{:S(2)}) async-start(f32[4,8,8,128]{3,2,0,1:T(8,128)} %copy.71), calls=%async_computation.3 | async-start | bytes 262144 | tf_op jit(solution)/shard_map/all_to_all | solution.py:292
  411.5 156.7 %all-to-all-start.6 = ((bf16[32,128,512]{2,1,0:T(8,128)(2,1)}), bf16[32,128,512]{2,1,0:T(8,128)(2,1)}, u32[]{:S(2)}, u32[]{:S(2)}) async-start(bf16[32,128,512]{2,1,0:T(8,128)(2,1)} %get-tuple-element.13), calls=%async_computation.6 | async-start | bytes 8388608 | tf_op jit(solution)/shard_map/all_to_all | solution.py:409
  449.9 13.7 %collective-permute-start.20 = (bf16[2,128,512]{2,1,0:T(8,128)(2,1)S(1)}, bf16[2,128,512]{2,1,0:T(8,128)(2,1)S(1)}, u32[]{:S(2)}, u32[]{:S(2)}) collective-permute-start(bf16[2,128,512]{2,1,0:T(8,128)(2,1)S(1)} %get-tuple-element.46), channel_id=1, source_target_pairs={{0,8},{8,16},{16,24},{24,0},{1,9},{9,17},{17,25},{25,1},{2,10},{10... | collective-permute-start | bytes 786440 | tf_op jit(solution)/shard_map/ppermute | solution.py:431
  451.1 12.4 %collective-permute-start.22 = (bf16[2,128,512]{2,1,0:T(8,128)(2,1)S(1)}, bf16[2,128,512]{2,1,0:T(8,128)(2,1)S(1)}, u32[]{:S(2)}, u32[]{:S(2)}) collective-permute-start(bf16[2,128,512]{2,1,0:T(8,128)(2,1)S(1)} %get-tuple-element.47), channel_id=1, source_target_pairs={{0,24},{8,0},{16,8},{24,16},{1,25},{9,1},{17,9},{25,17},{2,26},{10... | collective-permute-start | bytes 786440 | tf_op jit(solution)/shard_map/ppermute | solution.py:431
  452.7 10.9 %collective-permute-start.21 = (bf16[2,128,512]{2,1,0:T(8,128)(2,1)S(1)}, bf16[2,128,512]{2,1,0:T(8,128)(2,1)S(1)}, u32[]{:S(2)}, u32[]{:S(2)}) collective-permute-start(bf16[2,128,512]{2,1,0:T(8,128)(2,1)S(1)} %get-tuple-element.48), channel_id=1, source_target_pairs={{0,16},{8,24},{16,0},{24,8},{1,17},{9,25},{17,1},{25,9},{2,18},{10... | collective-permute-start | bytes 786440 | tf_op jit(solution)/shard_map/ppermute | solution.py:431
  464.6 52.3 %collective-permute-start.23 = (f32[2,128,512]{2,1,0:T(8,128)S(1)}, f32[2,128,512]{2,1,0:T(8,128)S(1)}, u32[]{:S(2)}, u32[]{:S(2)}) collective-permute-start(f32[2,128,512]{2,1,0:T(8,128)S(1)} %fusion.1), channel_id=1, source_target_pairs={{32,0},{96,64},{160,128},{224,192},{33,1},{97,65},{161,129},{225,1... | collective-permute-start | bytes 1572872 | tf_op jit(solution)/shard_map/ppermute | solution.py:435
  517.1 11.9 %collective-permute-start.24 = (f32[2,128,512]{2,1,0:T(8,128)S(1)}, f32[2,128,512]{2,1,0:T(8,128)S(1)}, u32[]{:S(2)}, u32[]{:S(2)}) collective-permute-start(f32[2,128,512]{2,1,0:T(8,128)S(1)} %add.255), channel_id=1, source_target_pairs={{64,0},{192,128},{65,1},{193,129},{66,2},{194,130},{67,3},{195,131... | collective-permute-start | bytes 1572872 | tf_op jit(solution)/shard_map/ppermute | solution.py:435
  529.0 13.8 %collective-permute-start.25 = (f32[2,128,512]{2,1,0:T(8,128)S(1)}, f32[2,128,512]{2,1,0:T(8,128)S(1)}, u32[]{:S(2)}, u32[]{:S(2)}) collective-permute-start(f32[2,128,512]{2,1,0:T(8,128)S(1)} %add.256), channel_id=1, source_target_pairs={{128,0},{129,1},{130,2},{131,3},{132,4},{133,5},{134,6},{135,7},{1... | collective-permute-start | bytes 1572872 | tf_op jit(solution)/shard_map/ppermute | solution.py:435
  530.3 16.5 %collective-permute-start.19 = (bf16[2,128,512]{2,1,0:T(8,128)(2,1)S(1)}, bf16[2,128,512]{2,1,0:T(8,128)(2,1)S(1)}, u32[]{:S(2)}, u32[]{:S(2)}) collective-permute-start(bf16[2,128,512]{2,1,0:T(8,128)(2,1)S(1)} %get-tuple-element.49), channel_id=1, source_target_pairs={{8,0},{16,8},{24,16},{32,24},{40,32},{48,40},{56,48},{64,56},{72,6... | collective-permute-start | bytes 786440 | tf_op jit(solution)/shard_map/ppermute | solution.py:427
  530.4 16.5 %collective-permute-start.18 = (bf16[2,128,512]{2,1,0:T(8,128)(2,1)S(1)}, bf16[2,128,512]{2,1,0:T(8,128)(2,1)S(1)}, u32[]{:S(2)}, u32[]{:S(2)}) collective-permute-start(bf16[2,128,512]{2,1,0:T(8,128)(2,1)S(1)} %get-tuple-element.50), channel_id=1, source_target_pairs={{0,8},{8,16},{16,24},{24,32},{32,40},{40,48},{48,56},{56,64},{64,7... | collective-permute-start | bytes 786440 | tf_op jit(solution)/shard_map/ppermute | solution.py:426
  542.9 15.3 %copy-start.2 = (bf16[2,128,512]{2,1,0:T(8,128)(2,1)}, bf16[2,128,512]{2,1,0:T(8,128)(2,1)S(1)}, u32[]{:S(2)}) copy-start(bf16[2,128,512]{2,1,0:T(8,128)(2,1)S(1)} %add_convert_fusion.s0_ref) | copy-start | bytes 786436
  543.0 15.2 %collective-permute-start.28 = (bf16[2,128,512]{2,1,0:T(8,128)(2,1)S(1)}, bf16[2,128,512]{2,1,0:T(8,128)(2,1)S(1)}, u32[]{:S(2)}, u32[]{:S(2)}) collective-permute-start(bf16[2,128,512]{2,1,0:T(8,128)(2,1)S(1)} %add_convert_fusion.s0_ref), channel_id=1, source_target_pairs={{24,0},{25,1},{26,2},{27,3},{28,4},{29,5},{30,6},{31,7}} | collective-permute-start | bytes 786440 | tf_op jit(solution)/shard_map/ppermute | solution.py:438
  544.3 13.9 %collective-permute-start.27 = (bf16[2,128,512]{2,1,0:T(8,128)(2,1)S(1)}, bf16[2,128,512]{2,1,0:T(8,128)(2,1)S(1)}, u32[]{:S(2)}, u32[]{:S(2)}) collective-permute-start(bf16[2,128,512]{2,1,0:T(8,128)(2,1)S(1)} %add_convert_fusion.s0_ref), channel_id=1, source_target_pairs={{16,0},{17,1},{18,2},{19,3},{20,4},{21,5},{22,6},{23,7}} | collective-permute-start | bytes 786440 | tf_op jit(solution)/shard_map/ppermute | solution.py:438
  545.6 12.6 %collective-permute-start.26 = (bf16[2,128,512]{2,1,0:T(8,128)(2,1)S(1)}, bf16[2,128,512]{2,1,0:T(8,128)(2,1)S(1)}, u32[]{:S(2)}, u32[]{:S(2)}) collective-permute-start(bf16[2,128,512]{2,1,0:T(8,128)(2,1)S(1)} %add_convert_fusion.s0_ref), channel_id=1, source_target_pairs={{8,0},{9,1},{10,2},{11,3},{12,4},{13,5},{14,6},{15,7}} | collective-permute-start | bytes 786440 | tf_op jit(solution)/shard_map/ppermute | solution.py:438
  546.9 11.4 %copy-start.11 = (bf16[2,128,512]{2,1,0:T(8,128)(2,1)}, bf16[2,128,512]{2,1,0:T(8,128)(2,1)S(1)}, u32[]{:S(2)}) copy-start(bf16[2,128,512]{2,1,0:T(8,128)(2,1)S(1)} %collective-permute-done.19.right_ref) | copy-start | bytes 786436
  546.9 11.3 %copy-start.12 = (bf16[2,128,512]{2,1,0:T(8,128)(2,1)}, bf16[2,128,512]{2,1,0:T(8,128)(2,1)S(1)}, u32[]{:S(2)}) copy-start(bf16[2,128,512]{2,1,0:T(8,128)(2,1)S(1)} %collective-permute-done.18.left_ref) | copy-start | bytes 786436
  558.2 0.7 copy-start.14
  558.2 0.8 copy-start.16
  558.2 0.9 copy-start.17
  568.3 37.7 %all-to-all-start.8 = ((bf16[8,2,128,512]{3,2,1,0:T(8,128)(2,1)}), bf16[8,2,128,512]{3,2,1,0:T(8,128)(2,1)S(1)}, u32[]{:S(2)}, u32[]{:S(2)}) async-start(bf16[8,2,128,512]{3,2,1,0:T(8,128)(2,1)} %shard_map.103), calls=%async_computation.8 | async-start | bytes 4194304 | tf_op jit(solution)/shard_map/all_to_all | solution.py:449
  606.0 19.5 %all-to-all-start.7 = ((bf16[8,128,512]{2,1,0:T(8,128)(2,1)}), bf16[8,128,512]{2,1,0:T(8,128)(2,1)S(1)}, u32[]{:S(2)}, u32[]{:S(2)}) async-start(bf16[8,128,512]{2,1,0:T(8,128)(2,1)} %shard_map.102), calls=%async_computation.7 | async-start | bytes 2097152 | tf_op jit(solution)/shard_map/all_to_all | solution.py:463
  611.9 3.0 copy-start.1

commit v2 on v1

v2 whole, which is shorter than its diff:
```python
from functools import partial

import jax
import jax.numpy as jnp
from jax import lax
from jax.experimental import pallas as pl
from jax.experimental.pallas import tpu as pltpu
from jax.sharding import Mesh, PartitionSpec as P

HEAD_DIM = 128
BLOCK = 128
RAND = 3
GLOB = 2
NGLOB = 4
NX = 4
SLOTS = 3 + GLOB
BF16 = jnp.bfloat16
F32 = jnp.float32
VMEM_LIMIT = 58 * 1024 * 1024
SCALE = HEAD_DIM ** (-0.5)
CTX = ("z", "x")
PER_STEP = 4
GROUP = 8
PARTS = 4
FAR = 1e30


def dot_nt(a, b):
    return lax.dot_general(a, b, (((1,), (1,)), ((), ())), preferred_element_type=F32)


def dot_nn(a, b):
    return lax.dot_general(a, b, (((1,), (0,)), ((), ())), preferred_element_type=F32)


def dot_tn(a, b):
    return lax.dot_general(a, b, (((0,), (0,)), ((), ())), preferred_element_type=F32)


def params():
    return pltpu.CompilerParams(vmem_limit_bytes=VMEM_LIMIT)


def whole(shape):
    return pl.BlockSpec(shape, lambda *_: (0,) * len(shape))


def call(body, grid, scalars, ins, in_specs, out_shape, out_specs, scratch=()):
    return pl.pallas_call(
        body,
        grid_spec=pltpu.PrefetchScalarGridSpec(
            num_scalar_prefetch=len(scalars),
            grid=grid,
            in_specs=in_specs,
            out_specs=out_specs,
            scratch_shapes=list(scratch),
        ),
        out_shape=out_shape,
        compiler_params=params(),
    )(*scalars, *ins)


def pick_body(count, row_ref, x_ref, o_ref, sems):
    copies = [
        pltpu.make_async_copy(x_ref.at[row_ref[i]], o_ref.at[i], sems.at[i]) for i in range(count)
    ]
    for copy in copies:
        copy.start()
    for copy in copies:
        copy.wait()


def pick_rows(rows_of, x, count):
    return call(
        partial(pick_body, count),
        (1,),
        (rows_of,),
        (x,),
        [whole(x.shape)],
        jax.ShapeDtypeStruct((count,) + x.shape[1:], x.dtype),
        pl.BlockSpec(memory_space=pl.ANY),
        [pltpu.SemaphoreType.DMA((count,))],
    )


def cut_body(count, place_ref, a_ref, b_ref, *outs):
    features = a_ref.shape[1] // count
    for s in range(count):
        start = pl.multiple_of(place_ref[s] * features, features)
        outs[s][0] = a_ref[:, pl.ds(start, features)]
        outs[s][1] = b_ref[:, pl.ds(start, features)]


def cut(places, a, b, count):
    unit = (2, a.shape[0], a.shape[1] // count)
    return call(
        partial(cut_body, count),
        (1,),
        (places,),
        (a, b),
        [whole(a.shape)] * 2,
        [jax.ShapeDtypeStruct(unit, a.dtype)] * count,
        [whole(unit)] * count,
    )


def joined_body(count, place_ref, *refs):
    a_ref, b_ref = refs[count:]
    features = a_ref.shape[1] // count
    for s in range(count):
        start = pl.multiple_of(place_ref[s] * features, features)
        a_ref[:, pl.ds(start, features)] = refs[s][0]
        b_ref[:, pl.ds(start, features)] = refs[s][1]


def joined(places, pieces):
    count = len(pieces)
    _, tokens, features = pieces[0].shape
    shape = (tokens, features * count)
    return call(
        partial(joined_body, count),
        (1,),
        (places,),
        pieces,
        [whole(pieces[0].shape)] * count,
        [jax.ShapeDtypeStruct(shape, pieces[0].dtype)] * 2,
        [whole(shape)] * 2,
    )


def order_body(count, place_ref, *refs):
    out = refs[count]
    for s in range(count):
        out[place_ref[s]] = refs[s][...]


def put_in_order(places, pieces):
    count = len(pieces)
    shape = pieces[0].shape
    return call(
        partial(order_body, count),
        (1,),
        (places,),
        pieces,
        [whole(shape)] * count,
        jax.ShapeDtypeStruct((count,) + shape, pieces[0].dtype),
        whole((count,) + shape),
    )


def extend_body(rows, kv_ref, left_ref, right_ref, out):
    out[0] = left_ref[...]
    for r in range(rows):
        out[1 + r] = kv_ref[r]
    out[rows + 1] = right_ref[...]


def extend(kv_rows, left, right):
    rows = kv_rows.shape[0]
    shape = left.shape
    full = (rows + 2,) + shape
    return call(
        partial(extend_body, rows),
        (1,),
        (),
        (kv_rows, left, right),
        [whole(kv_rows.shape)] + [whole(shape)] * 2,
        jax.ShapeDtypeStruct(full, kv_rows.dtype),
        whole(full),
    )


def columns(h):
    return slice(h * HEAD_DIM, (h + 1) * HEAD_DIM)


def row_stats(tiles):
    s = [masked(dot_nt(t[0], t[2]) * SCALE, t[4]) for t in tiles]
    dp = [dot_nt(t[1], t[3]) for t in tiles]
    top = [jnp.max(a, axis=0, keepdims=True) for a in s]
    p = [jnp.exp(a - m) for a, m in zip(s, top)]
    total = [jnp.sum(a, axis=0, keepdims=True) for a in p]
    mean = [jnp.sum(a * b, axis=0, keepdims=True) / n for a, b, n in zip(p, dp, total)]
    return [(m + jnp.log(n), x) for m, n, x in zip(top, total, mean)]


def groups(items, size):
    return [items[i : i + size] for i in range(0, len(items), size)]


def masked(s, masks):
    if masks is None:
        return s
    parts = [s[j * BLOCK : (j + 1) * BLOCK] for j in range(len(masks))]
    parts = [x if m is None else jnp.where(m, -jnp.inf, x) for x, m in zip(parts, masks)]
    return jnp.concatenate(parts, 0) if len(parts) > 1 else parts[0]


def stacked(kv_ref, slots, t, cols):
    return jnp.concatenate([kv_ref[j, t, :, cols] for j in slots], 0)


def band_stats_body(rows, heads, edge_ref, x_ref, kv_ref, o_ref):
    row = pl.program_id(0)
    off_left = (row == 0) & (edge_ref[0] != 0)
    off_right = (row == rows - 1) & (edge_ref[1] != 0)
    slots = [row, row + 1, row + 2]
    for some in groups(range(heads), 2):
        tiles = [
            (
                stacked(kv_ref, slots, 0, columns(h)),
                stacked(kv_ref, slots, 1, columns(h)),
                x_ref[0, 0, :, columns(h)],
                x_ref[0, 1, :, columns(h)],
                [off_left, None, off_right],
            )
            for h in some
        ]
        for h, (log, mean) in zip(some, row_stats(tiles)):
            o_ref[0, h : h + 1, :] = log
            o_ref[0, heads + h : heads + h + 1, :] = mean


def summary_stats_body(rows, heads, slot_ref, x_ref, kv_ref, o_ref):
    row = pl.program_id(0)
    slots = [slot_ref[row * GLOB + j] for j in range(GLOB)]
    for some in groups(range(heads), 4):
        tiles = [
            (
                stacked(kv_ref, slots, 0, columns(h)),
                stacked(kv_ref, slots, 1, columns(h)),
                x_ref[0, 0, :, columns(h)],
                x_ref[0, 1, :, columns(h)],
                None,
            )
            for h in some
        ]
        for h, (log, mean) in zip(some, row_stats(tiles)):
            o_ref[0, h : h + 1, :] = log
            o_ref[0, heads + h : heads + h + 1, :] = mean


def place_of(e, nz):
    return (e % NX) * nz + e // NX


def entry_tiles(heads):
    return groups([(i, h) for i in range(PER_STEP) for h in range(heads)], GROUP)


def entry_stats_body(heads, nz, own_ref, x_ref, kv_ref, o_ref):
    base = pl.program_id(0) * PER_STEP
    for some in entry_tiles(heads):
        tiles = [
            (
                kv_ref[own_ref[base + i], 0, :, columns(h)],
                kv_ref[own_ref[base + i], 1, :, columns(h)],
                x_ref[i, 0, :, columns(h)],
                x_ref[i, 1, :, columns(h)],
                None,
            )
            for i, h in some
        ]
        for (i, h), (log, mean) in zip(some, row_stats(tiles)):
            place = place_of(base + i, nz)
            o_ref[place, h : h + 1, :] = log
            o_ref[place, heads + h : heads + h + 1, :] = mean


def combine_body(
    rows, heads, count, nz, owner_ref, row_ref, band_ref, sum_ref, rem_ref, ld_ref, out_ref
):
    for r in range(rows):
        parts = [band_ref[r], sum_ref[r]]
        for j in range(RAND):
            o = owner_ref[r * RAND + j]
            parts.append(rem_ref[place_of(o, nz)])
        logs = [p[:heads] for p in parts]
        means = [p[heads:] for p in parts]
        top = logs[0]
        for x in logs[1:]:
            top = jnp.maximum(top, x)
        weights = [jnp.exp(x - top) for x in logs]
        total = sum(weights[1:], weights[0])
        mean = sum([w * m for w, m in zip(weights[1:], means[1:])], weights[0] * means[0])
        ld_ref[r, :heads] = top + jnp.log(total)
        ld_ref[r, heads:] = mean / total
    for o in range(count):
        out_ref[place_of(o, nz)] = ld_ref[row_ref[o]]


def pairs(tiles):
    s = [masked(dot_nt(t[0], t[2]) * SCALE, t[6]) for t in tiles]
    dp = [dot_nt(t[1], t[3]) for t in tiles]
    p = [jnp.exp(a - t[4]) for a, t in zip(s, tiles)]
    ds = [(a * (b - t[5])).astype(BF16) for a, b, t in zip(p, dp, tiles)]
    return [a.astype(BF16) for a in p], ds


def grads(tiles):
    p, ds = pairs(tiles)
    dk = [dot_nn(a, t[2]) for a, t in zip(ds, tiles)]
    dv = [dot_nn(a, t[3]) for a, t in zip(p, tiles)]
    dq = [dot_tn(a, t[0]) for a, t in zip(ds, tiles)]
    return zip(dk, dv, dq)


def entry_queries_body(heads, nz, part, own_ref, valid_ref, x_ref, ld_ref, kv_ref, *refs):
    dq_ref, pair_ref = refs[-2:]
    base = (part * pl.num_programs(0) + pl.program_id(0)) * PER_STEP
    far = [jnp.where(valid_ref[base + i] != 0, 0.0, FAR) for i in range(PER_STEP)]
    place = [place_of(base + i, nz) for i in range(PER_STEP)]
    for some in entry_tiles(heads):
        tiles = [
            (
                kv_ref[own_ref[base + i], 0, :, columns(h)],
                kv_ref[own_ref[base + i], 1, :, columns(h)],
                x_ref[i, 0, :, columns(h)],
                x_ref[i, 1, :, columns(h)],
                ld_ref[place[i], h : h + 1, :] + far[i],
                ld_ref[place[i], heads + h : heads + h + 1, :],
                None,
            )
            for i, h in some
        ]
        p, ds = pairs(tiles)
        for (i, h), a, b in zip(some, p, ds):
            pair_ref[i, 0, h] = b
            pair_ref[i, 1, h] = a
        dq = [dot_tn(a, t[0]) for a, t in zip(ds, tiles)]
        for (i, h), a in zip(some, dq):
            dq_ref[i, :, columns(h)] = (a * SCALE).astype(BF16)


def entry_keys_body(heads, own_ref, x_ref, pair_ref, acc_ref):
    step = pl.program_id(0)

    @pl.when(step == 0)
    def _():
        acc_ref[...] = jnp.zeros_like(acc_ref)

    for i in range(PER_STEP):
        own = own_ref[step * PER_STEP + i]
        tiles = [(t, h) for t in range(2) for h in range(heads)]
        terms = [dot_nn(pair_ref[i, t, h], x_ref[i, t, :, columns(h)]) for t, h in tiles]
        for (t, h), term in zip(tiles, terms):
            acc_ref[own, t, :, columns(h)] += term


def row_tile(x_ref, ld_ref, heads, h, keys, vals, masks):
    return (
        keys,
        vals,
        x_ref[0, 0, :, columns(h)],
        x_ref[0, 1, :, columns(h)],
        ld_ref[0, h : h + 1, :],
        ld_ref[0, heads + h : heads + h + 1, :],
        masks,
    )


def early_grads_body(
    rows, heads, slot_ref, edge_ref, x_ref, ld_ref, sum_ref, left_ref, right_ref, *refs
):
    dq_ref, side_ref, acc_ref = refs
    row = pl.program_id(0)

    @pl.when(row == 0)
    def _():
        acc_ref[...] = jnp.zeros_like(acc_ref)

    slots = [slot_ref[row * GLOB + j] for j in range(GLOB)]
    tile = partial(row_tile, x_ref, ld_ref, heads)
    for some in groups(range(heads), 4):
        tiles = [
            tile(h, stacked(sum_ref, slots, 0, columns(h)), stacked(sum_ref, slots, 1, columns(h)), None)
            for h in some
        ]
        for h, (dk, dv, dq) in zip(some, grads(tiles)):
            dq_ref[0, :, columns(h)] = dq
            for n, j in enumerate(slots):
                acc_ref[j, 0, :, columns(h)] += dk[n * BLOCK : (n + 1) * BLOCK]
                acc_ref[j, 1, :, columns(h)] += dv[n * BLOCK : (n + 1) * BLOCK]

    def at_edge(source_ref, off, place):
        for some in groups(range(heads), 4):
            tiles = [
                tile(h, source_ref[0, :, columns(h)], source_ref[1, :, columns(h)], [off])
                for h in some
            ]
            for h, (dk, dv, dq) in zip(some, grads(tiles)):
                dq_ref[0, :, columns(h)] += dq
                side_ref[place, 0, :, columns(h)] = (dk * SCALE).astype(BF16)
                side_ref[place, 1, :, columns(h)] = dv.astype(BF16)

    @pl.when(row == 0)
    def _():
        at_edge(left_ref, edge_ref[0] != 0, 0)

    @pl.when(row == rows - 1)
    def _():
        at_edge(right_ref, edge_ref[1] != 0, 1)
        for n in range(NGLOB):
            side_ref[2 + n, 0] = (acc_ref[n, 0] * SCALE).astype(BF16)
            side_ref[2 + n, 1] = acc_ref[n, 1].astype(BF16)


def late_grads_body(rows, heads, x_ref, ld_ref, kv_ref, begun_ref, dq_ref, acc_ref):
    row = pl.program_id(0)

    @pl.when(row == 0)
    def _():
        acc_ref[...] = jnp.zeros_like(acc_ref)

    slots = [row, row + 1, row + 2]
    masks = [row == 0, None, row == rows - 1]
    tile = partial(row_tile, x_ref, ld_ref, heads)
    for some in groups(range(heads), 2):
        tiles = [
            tile(h, stacked(kv_ref, slots, 0, columns(h)), stacked(kv_ref, slots, 1, columns(h)), masks)
            for h in some
        ]
        for h, (dk, dv, dq) in zip(some, grads(tiles)):
            dq_ref[0, :, columns(h)] = (dq + begun_ref[0, :, columns(h)]) * SCALE
            for n, j in enumerate(slots):
                acc_ref[j, 0, :, columns(h)] += dk[n * BLOCK : (n + 1) * BLOCK]
                acc_ref[j, 1, :, columns(h)] += dv[n * BLOCK : (n + 1) * BLOCK]


def finish_kv_body(rows, place_ref, first_ref, loc_ref, *refs):
    rand_ref, left_ref, right_ref = refs[:3]
    sums = refs[3 : 3 + NGLOB]
    outs = refs[3 + NGLOB :]
    for s in range(rows):
        row = place_ref[s]
        at_first = (row == 0).astype(F32)
        at_last = (row == rows - 1).astype(F32)
        for t in range(2):
            total = loc_ref[row + 1, t] + rand_ref[row, t]
            if t == 0:
                total = total * SCALE
            outs[s][t] = (
                total + at_first * left_ref[t].astype(F32) + at_last * right_ref[t].astype(F32)
            ).astype(BF16)
        for n, sum_ref in enumerate(sums):

            @pl.when((row == n) & (first_ref[0] != 0))
            def _(n=n, s=s, row=row, sum_ref=sum_ref, at_first=at_first, at_last=at_last):
                for t in range(2):
                    total = loc_ref[row + 1, t] + rand_ref[row, t]
                    if t == 0:
                        total = total * SCALE
                    total += at_first * left_ref[t].astype(F32)
                    total += at_last * right_ref[t].astype(F32)
                    outs[s][t] = (total + sum_ref[t].astype(F32)).astype(BF16)


def finish_q_body(rows, owner_ref, loc_ref, in_ref, o_ref):
    for r in range(rows):
        total = loc_ref[r]
        for j in range(RAND):
            total += in_ref[owner_ref[r * RAND + j]].astype(F32)
        o_ref[r] = total.astype(BF16)


def exchange_small(x):
    nz = lax.axis_size("z")
    x = x.reshape((NX, nz) + x.shape[1:])
    x = lax.all_to_all(x, "x", split_axis=0, concat_axis=0, tiled=True)
    x = lax.all_to_all(x, "z", split_axis=1, concat_axis=1, tiled=True)
    return x.reshape((NX * nz,) + x.shape[2:])


def ring(axis, shift):
    count = lax.axis_size(axis)
    return [(i, (i + shift) % count) for i in range(count)]


def on_device(query, keys, values, grad_out, random_owner, random_within, global_ids):
    nz = lax.axis_size("z")
    nh = lax.axis_size("head")
    zi = lax.axis_index("z")
    xi = lax.axis_index("x")
    hi = lax.axis_index("head")
    count = nz * NX
    ctx_index = zi * NX + xi
    tokens, width = query.shape
    features = width // nh
    heads = features // HEAD_DIM
    rows = nh
    unit = (2, BLOCK, features)
    stat = (2 * heads, BLOCK)
    shape = jax.ShapeDtypeStruct

    entries = rows * RAND
    owner_all = random_owner.reshape(count, entries)
    within_all = random_within.reshape(count, entries)
    hit = owner_all == ctx_index
    own = jnp.sum(jnp.where(hit, within_all, 0), axis=1).astype(jnp.int32)
    valid = jnp.any(hit, axis=1).astype(jnp.int32)
    owner_mine = lax.dynamic_index_in_dim(owner_all, ctx_index, 0, keepdims=False)
    named = owner_mine[:, None] == jnp.arange(count, dtype=jnp.int32)[None, :]
    entry_row = (jnp.arange(entries, dtype=jnp.int32) // RAND)[:, None]
    row_of = jnp.sum(jnp.where(named, entry_row, 0), axis=0).astype(jnp.int32)
    global_mine = lax.dynamic_slice_in_dim(global_ids, ctx_index * rows, rows, 0)
    slots = global_mine.reshape(-1)
    edges = jnp.stack([ctx_index == 0, ctx_index == count - 1]).astype(jnp.int32)
    heads_ids = jnp.arange(nh, dtype=jnp.int32)
    sent_to = (hi + heads_ids) % nh
    came_from = (hi - heads_ids) % nh

    x_split = jnp.stack(
        [
            query.reshape(BLOCK, nh, features).transpose(1, 0, 2),
            grad_out.reshape(BLOCK, nh, features).transpose(1, 0, 2),
        ],
        1,
    )
    x_rows = lax.all_to_all(x_split, "head", split_axis=0, concat_axis=0, tiled=True)

    x_sent = pick_rows(row_of, x_rows, count)
    x_sent, keys, values = lax.optimization_barrier((x_sent, keys, values))
    x_in = lax.all_to_all(x_sent, CTX, split_axis=0, concat_axis=0, tiled=True)

    kv_cut = cut(sent_to, keys, values, nh)
    pieces = [kv_cut[0]] + [lax.ppermute(kv_cut[s], "head", ring("head", s)) for s in range(1, nh)]
    kv_rows = put_in_order(came_from, pieces)
    left = lax.ppermute(kv_rows[rows - 1], CTX, [(i, (i + 1) % count) for i in range(count)])
    right = lax.ppermute(kv_rows[0], CTX, [((i + 1) % count, i) for i in range(count)])

    summary = kv_rows[0]
    for g in range(1, NGLOB):
        came = lax.ppermute(kv_rows[g], CTX, [(0, g)])
        summary = jnp.where(xi == g, came, summary)
    step = nz // 2
    while step:
        pairs = [(z, z + step) for z in range(0, nz, 2 * step)]
        came = lax.ppermute(summary, "z", pairs)
        summary = jnp.where(zi % (2 * step) == step, came, summary)
        step //= 2
    row_spec = pl.BlockSpec((1,) + unit, lambda i, *_: (i, 0, 0, 0))
    step_spec = pl.BlockSpec((PER_STEP,) + unit, lambda i, *_: (i, 0, 0, 0))
    stat_spec = pl.BlockSpec((1,) + stat, lambda i, *_: (i, 0, 0))
    half_spec = pl.BlockSpec((1, BLOCK, features), lambda i, *_: (i, 0, 0))

    stats_out = call(
        partial(entry_stats_body, heads, nz),
        (count // PER_STEP,),
        (own,),
        (x_in, kv_rows),
        [step_spec, whole(kv_rows.shape)],
        shape((count,) + stat, F32),
        whole((count,) + stat),
    )
    stats_out, left, right, summary = lax.optimization_barrier((stats_out, left, right, summary))
    kv_band = extend(kv_rows, left, right)
    summaries = [summary] + [lax.ppermute(summary, "x", ring("x", s)) for s in range(1, NX)]
    sum_places = (xi - jnp.arange(NX, dtype=jnp.int32)) % NX
    kv_sum = put_in_order(sum_places, summaries)
    stats_band = call(
        partial(band_stats_body, rows, heads),
        (rows,),
        (edges,),
        (x_rows, kv_band),
        [row_spec, whole(kv_band.shape)],
        shape((rows,) + stat, F32),
        stat_spec,
    )
    stats_sum = call(
        partial(summary_stats_body, rows, heads),
        (rows,),
        (slots,),
        (x_rows, kv_sum),
        [row_spec, whole(kv_sum.shape)],
        shape((rows,) + stat, F32),
        stat_spec,
    )
    stats_in = exchange_small(stats_out)
    ld, ld_out = call(
        partial(combine_body, rows, heads, count, nz),
        (1,),
        (owner_mine, row_of),
        (stats_band, stats_sum, stats_in),
        [whole(stats_band.shape)] * 2 + [whole(stats_in.shape)],
        (shape((rows,) + stat, F32), shape((count,) + stat, F32)),
        (whole((rows,) + stat), whole((count,) + stat)),
    )
    ld_in = exchange_small(ld_out)

    side_count = 2 + NGLOB
    dq_early, side = call(
        partial(early_grads_body, rows, heads),
        (rows,),
        (slots, edges),
        (x_rows, ld, kv_sum, left, right),
        [row_spec, stat_spec, whole(kv_sum.shape), whole(unit), whole(unit)],
        (shape((rows, BLOCK, features), F32), shape((side_count,) + unit, BF16)),
        (half_spec, whole((side_count,) + unit)),
        [pltpu.VMEM((NGLOB,) + unit, F32)],
    )
    ld_in, side = lax.optimization_barrier((ld_in, side))
    from_left = lax.ppermute(side[1], CTX, [(i, (i + 1) % count) for i in range(count)])
    from_right = lax.ppermute(side[0], CTX, [((i + 1) % count, i) for i in range(count)])
    summed = lax.dynamic_index_in_dim(side, 2 + xi, 0, keepdims=False).astype(F32)
    for s in range(1, NX):
        sent = lax.dynamic_index_in_dim(side, 2 + (xi + s) % NX, 0, keepdims=False)
        summed = summed + lax.ppermute(sent, "x", ring("x", s)).astype(F32)
    part_steps = count // PER_STEP // PARTS
    dq_out = pairs_out = None
    hop = 1
    for part in range(PARTS):

        def at_part(i, *_, part=part):
            return (part * part_steps + i, 0, 0, 0)

        def half_part(i, *_, part=part):
            return (part * part_steps + i, 0, 0)

        def pair_part(i, *_, part=part):
            return (part * part_steps + i, 0, 0, 0, 0)

        pair_shape = (2, heads, BLOCK, BLOCK)
        dq_out, pairs_out = pl.pallas_call(
            partial(entry_queries_body, heads, nz, part),
            grid_spec=pltpu.PrefetchScalarGridSpec(
                num_scalar_prefetch=2,
                grid=(part_steps,),
                in_specs=[
                    pl.BlockSpec((PER_STEP,) + unit, at_part),
                    whole((count,) + stat),
                    whole(kv_rows.shape),
                ]
                + ([pl.BlockSpec(memory_space=pl.ANY)] * 2 if part else []),
                out_specs=(
                    pl.BlockSpec((PER_STEP, BLOCK, features), half_part),
                    pl.BlockSpec((PER_STEP,) + pair_shape, pair_part),
                ),
            ),
            out_shape=(
                shape((count, BLOCK, features), BF16),
                shape((count,) + pair_shape, BF16),
            ),
            input_output_aliases={5: 0, 6: 1} if part else {},
            compiler_params=params(),
        )(own, valid, x_in, ld_in, kv_rows, *([dq_out, pairs_out] if part else []))
        dq_out, summed = lax.optimization_barrier((dq_out, summed))
        if hop < nz:
            links = [(z + hop, z) for z in range(0, nz, 2 * hop)]
            summed = summed + lax.ppermute(summed.astype(BF16), "z", links).astype(F32)
            hop *= 2
    dq_out, summed, from_left, from_right = lax.optimization_barrier(
        (dq_out, summed, from_left, from_right)
    )
    dq_in = lax.all_to_all(dq_out, CTX, split_axis=0, concat_axis=0, tiled=True)

    rand_acc = call(
        partial(entry_keys_body, heads),
        (count // PER_STEP,),
        (own,),
        (x_in, pairs_out),
        [step_spec, pl.BlockSpec((PER_STEP,) + pair_shape, lambda i, *_: (i, 0, 0, 0, 0))],
        shape((rows,) + unit, F32),
        whole((rows,) + unit),
    )
    total = summed.astype(BF16)
    totals = [total] + [lax.ppermute(total, CTX, [(g, 0)]) for g in range(1, NGLOB)]
    dq_loc, loc_acc = call(
        partial(late_grads_body, rows, heads),
        (rows,),
        (),
        (x_rows, ld, kv_band, dq_early),
        [row_spec, stat_spec, whole(kv_band.shape), half_spec],
        (shape((rows, BLOCK, features), F32), shape((rows + 2,) + unit, F32)),
        (half_spec, whole((rows + 2,) + unit)),
    )
    kv_back = call(
        partial(finish_kv_body, rows),
        (1,),
        (sent_to, edges),
        (loc_acc, rand_acc, from_left, from_right, *totals),
        [whole((rows + 2,) + unit), whole((rows,) + unit)] + [whole(unit)] * (2 + NGLOB),
        [shape(unit, BF16)] * rows,
        [whole(unit)] * rows,
    )
    kv_done = [kv_back[0]]
    for s in range(1, nh):
        kv_done.append(lax.ppermute(kv_back[s], "head", ring("head", s)))
    grad_keys, grad_values = joined(came_from, kv_done)
    dq_in, grad_keys, grad_values = lax.optimization_barrier((dq_in, grad_keys, grad_values))

    q_back = call(
        partial(finish_q_body, rows),
        (1,),
        (owner_mine,),
        (dq_loc, dq_in),
        [whole(dq_loc.shape), whole(dq_in.shape)],
        shape((rows, BLOCK, features), BF16),
        whole((rows, BLOCK, features)),
    )
    q_done = lax.all_to_all(q_back, "head", split_axis=0, concat_axis=0, tiled=True)
    return q_done.transpose(1, 0, 2).reshape(tokens, width), grad_keys, grad_values


def solution(mesh):
    count, nh = mesh.devices.shape
    fine = Mesh(mesh.devices.reshape(count // NX, NX, nh), ("z", "x", "head"))
    tokens = P(("z", "x", "head"), None)
    return jax.shard_map(
        on_device,
        mesh=fine,
        in_specs=(tokens,) * 4 + (P(),) * 3,
        out_specs=(tokens,) * 3,
        check_vma=False,
    )
```

time: 630 us -> 537 us (0.85)
  waiting for transfers between devices: 329 us -> 208 us
  starting transfers between devices: 97.7 us -> 140 us
  Pallas kernels: 144 us -> 128 us
    ppermute x10 -> x17, waiting for transfers between devices: 89.3 us -> 37.8 us  [the longest x7 18.8 us: on_device(): kv_done.append(lax.ppermute(kv_back[s], 'head', ring('head', s)))]
    pallas_call x10 -> x15, Pallas kernels: 144 us -> 103 us  [call(): pl.pallas_call(body, grid_spec=pltpu.PrefetchScalarGridSpec(num_scalar_pr...]
    ppermute x10 -> x17, starting transfers between devices: 14.4 us -> 52.1 us  [the longest x7 38.6 us: on_device(): kv_done.append(lax.ppermute(kv_back[s], 'head', ring('head', s)))]
    all_to_all x3 -> x1, waiting for transfers between devices: 53.6 us -> 25.5 us  [on_device(): lax.all_to_all(x_split, 'head', split_axis=0, concat_axis=0, tiled=True)]
    pallas_call x0 -> x4, Pallas kernels: none -> 24.7 us  [on_device(): pl.pallas_call(partial(entry_queries_body, heads, nz, part), grid_spec=pl...]
    ppermute x3, waiting for transfers between devices: 130 us -> 109 us  [on_device(): came = lax.ppermute(summary, 'z', pairs)]
    all_to_all x3 -> x1, starting transfers between devices: 22.6 us -> 6.88 us  [on_device(): lax.all_to_all(x_split, 'head', split_axis=0, concat_axis=0, tiled=True)]
    ppermute x3, waiting for transfers between devices: 20.7 us -> 36 us  [on_device(): came = lax.ppermute(kv_rows[g], CTX, [(0, g)])]
  transfers between devices with their start and end apart: 36 -> 42, of which waited for: 20 -> 15; matrix products, arithmetic and copies ran while one was open for 3% -> 2% of each run, Pallas kernels for 11% -> 22%
where the time goes in v2:
time: 537 us; the launch traced here: 531 us
  waiting for transfers between devices  208 us (39%)
  starting transfers between devices  140 us (26%)
  Pallas kernels  128 us (24%)
  blocking collectives  27.3 us (5%)
  local copies, waits for them, and re-layouts  17.9 us (3%)
  other arithmetic  8.31 us (2%)
    ppermute x3, waiting for transfers between devices, on_device(): came = lax.ppermute(summary, 'z', pairs)  109 us
    pallas_call x15, Pallas kernels, call(): pl.pallas_call(body, grid_spec=pltpu.PrefetchScalarGridSpec(num_scalar_pr...  103 us
    ppermute x7, starting transfers between devices, on_device(): kv_done.append(lax.ppermute(kv_back[s], 'head', ring('head', s)))  38.6 us
    ppermute x3, waiting for transfers between devices, on_device(): came = lax.ppermute(kv_rows[g], CTX, [(0, g)])  36 us
    all_to_all x1, waiting for transfers between devices, on_device(): lax.all_to_all(x_split, 'head', split_axis=0, concat_axis=0, tiled=True)  25.5 us
    pallas_call x4, Pallas kernels, on_device(): pl.pallas_call(partial(entry_queries_body, heads, nz, part), grid_spec=pl...  24.7 us
    all_to_all x1, blocking collectives, on_device(): lax.all_to_all(q_back, 'head', split_axis=0, concat_axis=0, tiled=True)  19.2 us
    ppermute x7, waiting for transfers between devices, on_device(): kv_done.append(lax.ppermute(kv_back[s], 'head', ring('head', s)))  18.8 us
  transfers between devices with their start and end apart: 42, of which 15 were waited for; matrix products, arithmetic and copies ran while one was open for 2% of the time, Pallas kernels for 22%

profile of v2, /device:TPU:1, one launch (start us, length us, event | category | flops | bytes accessed | tf_op | source)
XLA Modules:
  0.0 531.2 jit_solution(10595242797016264035)
XLA Ops:
  0.7 1.7 copy.50
  4.1 1.5 pad_maximum_fusion
  5.6 6.9 %all-to-all-start = ((bf16[8,2,128,512]{3,2,1,0:T(8,128)(2,1)}), bf16[8,2,128,512]{3,2,1,0:T(8,128)(2,1)S(1)}, u32[]{:S(2)}, u32[]{:S(2)}) async-start(bf16[8,2,128,512]{3,2,1,0:T(8,128)(2,1)} %pad_maximum_fusion), calls=%async_computation | async-start | bytes 4194304 | tf_op jit(solution)/shard_map/all_to_all | solution.py:519
  13.4 25.5 %all-to-all-done.x_ref = bf16[8,2,128,512]{3,2,1,0:T(8,128)(2,1)S(1)} async-done(((bf16[8,2,128,512]{3,2,1,0:T(8,128)(2,1)}), bf16[8,2,128,512]{3,2,1,0:T(8,128)(2,1)S(1)}, u32[]{:S(2)}, u32[]{:S(2)}) %all-to-all-start) | async-done | bytes 2097184 | tf_op jit(solution)/shard_map/all_to_all | solution.py:519
  38.9 1.4 copy-done.2
  40.2 5.8 %shard_map.94 = bf16[32,2,128,512]{3,2,1,0:T(8,128)(2,1)} custom-call(s32[32]{0:T(128)} %select_reduce_fusion.row_ref, bf16[8,2,128,512]{3,2,1,0:T(8,128)(2,1)} %copy-done.2), custom_call_target="tpu_custom_call" | custom-call | tf_op jit(solution)/shard_map/pallas_call | solution.py:49
  46.1 10.4 %all-to-all-start.1 = ((bf16[32,2,128,512]{3,2,1,0:T(8,128)(2,1)}), bf16[32,2,128,512]{3,2,1,0:T(8,128)(2,1)}, u32[]{:S(2)}, u32[]{:S(2)}) async-start(bf16[32,2,128,512]{3,2,1,0:T(8,128)(2,1)} %shard_map.94), calls=%async_computation.1 | async-start | bytes 16777216 | tf_op jit(solution)/shard_map/all_to_all | solution.py:523
  57.1 3.7 shard_map.95
  60.8 1.3 collective-permute-start
  62.1 2.1 collective-permute-start.2
  64.2 1.5 collective-permute-start.3
  65.7 2.6 collective-permute-start.4
  68.3 2.1 collective-permute-start.5
  70.4 6.9 %collective-permute-done.1.refs_2_ = bf16[2,128,512]{2,1,0:T(8,128)(2,1)S(1)} collective-permute-done((bf16[2,128,512]{2,1,0:T(8,128)(2,1)}, bf16[2,128,512]{2,1,0:T(8,128)(2,1)S(1)}, u32[]{:S(2)}, u32[]{:S(2)}) %collective-permute-start.1) | collective-permute-done | bytes 262176 | tf_op jit(solution)/shard_map/ppermute | solution.py:526
  77.9 10.7 %collective-permute-done.2.refs_3_ = bf16[2,128,512]{2,1,0:T(8,128)(2,1)S(1)} collective-permute-done((bf16[2,128,512]{2,1,0:T(8,128)(2,1)}, bf16[2,128,512]{2,1,0:T(8,128)(2,1)S(1)}, u32[]{:S(2)}, u32[]{:S(2)}) %collective-permute-start.2) | collective-permute-done | bytes 262176 | tf_op jit(solution)/shard_map/ppermute | solution.py:526
  90.2 3.6 shard_map.96.kv_ref
  93.8 1.4 slice_bitcast_fusion
  95.2 4.9 collective-permute-start.10
  100.1 1.3 collective-permute-start.11
  101.4 1.3 collective-permute-start.9
  102.7 14.1 %collective-permute-done.10 = bf16[2,128,512]{2,1,0:T(8,128)(2,1)S(1)} collective-permute-done((bf16[2,128,512]{2,1,0:T(8,128)(2,1)S(1)}, bf16[2,128,512]{2,1,0:T(8,128)(2,1)S(1)}, u32[]{:S(2)}, u32[]{:S(2)}) %collective-permute-start.10) | collective-permute-done | bytes 262176 | tf_op jit(solution)/shard_map/ppermute | solution.py:533
  116.8 21.8 %collective-permute-done.11 = bf16[2,128,512]{2,1,0:T(8,128)(2,1)S(1)} collective-permute-done((bf16[2,128,512]{2,1,0:T(8,128)(2,1)S(1)}, bf16[2,128,512]{2,1,0:T(8,128)(2,1)S(1)}, u32[]{:S(2)}, u32[]{:S(2)}) %collective-permute-start.11) | collective-permute-done | bytes 262176 | tf_op jit(solution)/shard_map/ppermute | solution.py:533
  139.7 1.3 collective-permute-start.12
  141.0 104.7 %collective-permute-done.12 = bf16[2,128,512]{2,1,0:T(8,128)(2,1)S(1)} collective-permute-done((bf16[2,128,512]{2,1,0:T(8,128)(2,1)S(1)}, bf16[2,128,512]{2,1,0:T(8,128)(2,1)S(1)}, u32[]{:S(2)}, u32[]{:S(2)}) %collective-permute-start.12) | collective-permute-done | bytes 262176 | tf_op jit(solution)/shard_map/ppermute | solution.py:538
  245.7 1.3 collective-permute-start.13
  247.1 4.1 collective-permute-done.13
  251.2 1.3 collective-permute-start.14
  252.6 4.8 collective-permute-start.8
  258.2 11.5 %shard_map.97 = f32[32,8,128]{2,1,0:T(8,128)} custom-call(s32[32]{0:T(128)} %reduce_sum.28.own_ref, bf16[32,2,128,512]{3,2,1,0:T(8,128)(2,1)} %all-to-all-done.1.x_ref, bf16[8,2,128,512]{3,2,1,0:T(8,128)(2,1)} %shard_map.96.kv_ref), custom_call_target="tpu_custom_call" | custom-call | tf_op jit(solution)/shard_map/pallas_call | solution.py:49
  269.8 4.5 all-to-all-start.2
  274.3 1.5 collective-permute-start.15
  275.7 2.4 collective-permute-start.16
  280.0 9.2 %all-to-all-start.3 = ((f32[4,8,8,128]{3,2,0,1:T(8,128)}), f32[4,8,8,128]{3,2,0,1:T(8,128)S(1)}, u32[]{:S(2)}, u32[]{:S(2)}) async-start(f32[4,8,8,128]{3,2,0,1:T(8,128)} %copy.55), calls=%async_computation.3 | async-start | bytes 262144 | tf_op jit(solution)/shard_map/all_to_all | solution.py:470
  291.1 3.4 shard_map.98.kv_ref
  294.6 8.6 %shard_map.99.band_ref = f32[8,8,128]{2,1,0:T(8,128)} custom-call(s32[2]{0:T(128)} %add_convert_fusion.edge_ref.first_ref, bf16[8,2,128,512]{3,2,1,0:T(8,128)(2,1)} %copy-done.2, bf16[10,2,128,512]{3,2,1,0:T(8,128)(2,1)} %shard_map.98.kv_ref), custom_call_target="tpu_custom_call" | custom-call | tf_op jit(solution)/shard_map/pallas_call | solution.py:49
  304.6 2.9 shard_map.100.kv_ref.sum_ref
  307.5 7.6 %shard_map.101.sum_ref = f32[8,8,128]{2,1,0:T(8,128)} custom-call(s32[16]{0:T(128)} %reshape.56.slot_ref, bf16[8,2,128,512]{3,2,1,0:T(8,128)(2,1)} %copy-done.2, bf16[4,2,128,512]{3,2,1,0:T(8,128)(2,1)} %shard_map.100.kv_ref.sum_ref), custom_call_target="tpu_custom_call" | custom-call | tf_op jit(solution)/shard_map/pallas_call | solution.py:49
  315.8 2.4 shard_map.102
  318.3 8.1 %all_to_all.40 = f32[4,8,8,128]{3,2,1,0:T(8,128)S(1)} all-to-all(f32[4,8,8,128]{3,2,1,0:T(8,128)} %bitcast.55), channel_id=1, replica_groups=mesh['z'=8,'x'=4,'head'=8] {'x'}, dimensions={0} | all-to-all | bytes 262144 | tf_op jit(solution)/shard_map/all_to_all | solution.py:469
  327.0 6.6 %all-to-all-start.5 = ((f32[4,8,8,128]{3,2,0,1:T(8,128)}), f32[4,8,8,128]{3,2,0,1:T(8,128)S(1)}, u32[]{:S(2)}, u32[]{:S(2)}) async-start(f32[4,8,8,128]{3,2,0,1:T(8,128)} %copy.57), calls=%async_computation.5 | async-start | bytes 262144 | tf_op jit(solution)/shard_map/all_to_all | solution.py:470
  333.6 11.3 %shard_map.103 = (f32[8,128,512]{2,1,0:T(8,128)}, bf16[6,2,128,512]{3,2,1,0:T(8,128)(2,1)}) custom-call(s32[16]{0:T(128)} %reshape.56.slot_ref, s32[2]{0:T(128)} %add_convert_fusion.edge_ref.first_ref, bf16[8,2,128,512]{3,2,1,0:T(8,128)(2,1)} %copy-done.2, f32[8,8,128]{2,1,0:T(8,128)} %get-tuple-element.74.ld_ref, ...), custom_call_target="tpu_custom_call" | custom-call | tf_op jit(solution)/shard_map/pallas_call | solution.py:49
  345.6 1.4 slice_bitcast_fusion.5
  347.3 1.8 collective-permute-start.19
  350.6 6.1 %shard_map.105 = (bf16[32,128,512]{2,1,0:T(8,128)(2,1)}, bf16[32,2,4,128,128]{4,3,2,1,0:T(8,128)(2,1)}) custom-call(s32[32]{0:T(128)} %reduce_sum.28.own_ref, s32[32]{0:T(128)} %convert_element_type.43.valid_ref, bf16[32,2,128,512]{3,2,1,0:T(8,128)(2,1)} %all-to-all-done.1.x_ref, f32[32,8,128]{2,1,0:T(8,128)} %bitcast.49, ...), custom_call_target="tpu_custom_call" | custom-call | tf_op jit(solution)/shard_map/pallas_call | solution.py:623
  359.4 6.2 %shard_map.106 = (bf16[32,128,512]{2,1,0:T(8,128)(2,1)}, bf16[32,2,4,128,128]{4,3,2,1,0:T(8,128)(2,1)}) custom-call(s32[32]{0:T(128)} %reduce_sum.28.own_ref, s32[32]{0:T(128)} %convert_element_type.43.valid_ref, bf16[32,2,128,512]{3,2,1,0:T(8,128)(2,1)} %all-to-all-done.1.x_ref, ...), custom_call_target="tpu_custom_call", output_to_operand_aliasing={{0}: (5, {}), {1}: (6, {})} | custom-call | tf_op jit(solution)/shard_map/pallas_call | solution.py:623
  367.0 6.2 %shard_map.107 = (bf16[32,128,512]{2,1,0:T(8,128)(2,1)}, bf16[32,2,4,128,128]{4,3,2,1,0:T(8,128)(2,1)}) custom-call(s32[32]{0:T(128)} %reduce_sum.28.own_ref, s32[32]{0:T(128)} %convert_element_type.43.valid_ref, bf16[32,2,128,512]{3,2,1,0:T(8,128)(2,1)} %all-to-all-done.1.x_ref, ...), custom_call_target="tpu_custom_call", output_to_operand_aliasing={{0}: (5, {}), {1}: (6, {})} | custom-call | tf_op jit(solution)/shard_map/pallas_call | solution.py:623
  375.9 4.2 collective-permute-start.25
  380.0 6.2 %shard_map.108 = (bf16[32,128,512]{2,1,0:T(8,128)(2,1)}, bf16[32,2,4,128,128]{4,3,2,1,0:T(8,128)(2,1)}) custom-call(s32[32]{0:T(128)} %reduce_sum.28.own_ref, s32[32]{0:T(128)} %convert_element_type.43.valid_ref, bf16[32,2,128,512]{3,2,1,0:T(8,128)(2,1)} %all-to-all-done.1.x_ref, ...), custom_call_target="tpu_custom_call", output_to_operand_aliasing={{0}: (5, {}), {1}: (6, {})} | custom-call | tf_op jit(solution)/shard_map/pallas_call | solution.py:623
  387.2 7.8 %all-to-all-start.6 = ((bf16[32,128,512]{2,1,0:T(8,128)(2,1)}), bf16[32,128,512]{2,1,0:T(8,128)(2,1)}, u32[]{:S(2)}, u32[]{:S(2)}) async-start(bf16[32,128,512]{2,1,0:T(8,128)(2,1)} %get-tuple-element.96), calls=%async_computation.6 | async-start | bytes 8388608 | tf_op jit(solution)/shard_map/all_to_all | solution.py:654
  397.6 11.2 %collective-permute-start.28 = (bf16[2,128,512]{2,1,0:T(8,128)(2,1)S(1)}, bf16[2,128,512]{2,1,0:T(8,128)(2,1)S(1)}, u32[]{:S(2)}, u32[]{:S(2)}) collective-permute-start(bf16[2,128,512]{2,1,0:T(8,128)(2,1)S(1)} %convert_add_fusion.1.refs_3_), channel_id=1, source_target_pairs={{24,0},{25,1},{26,2},{27,3},{28,4},{29,5},{30,6},{31,7}} | collective-permute-start | bytes 786440 | tf_op jit(solution)/shard_map/ppermute | solution.py:666
  408.8 12.8 %shard_map.104 = (f32[8,128,512]{2,1,0:T(8,128)}, f32[10,2,128,512]{3,2,1,0:T(8,128)}) custom-call(bf16[8,2,128,512]{3,2,1,0:T(8,128)(2,1)} %copy-done.2, f32[8,8,128]{2,1,0:T(8,128)} %get-tuple-element.74.ld_ref, bf16[10,2,128,512]{3,2,1,0:T(8,128)(2,1)} %shard_map.98.kv_ref, f32[8,128,512]{2,1,0:T(8,128)} %get-tuple-element.75.begun_ref), custom_call_target="tpu_custom_call" | custom-call | tf_op jit(solution)/shard_map/pallas_call | solution.py:49
  421.7 12.3 %shard_map.109.refs_0_ = f32[8,2,128,512]{3,2,1,0:T(8,128)} custom-call(s32[32]{0:T(128)} %reduce_sum.28.own_ref, bf16[32,2,128,512]{3,2,1,0:T(8,128)(2,1)} %all-to-all-done.1.x_ref, bf16[32,2,4,128,128]{4,3,2,1,0:T(8,128)(2,1)} %get-tuple-element.98.pair_ref), custom_call_target="tpu_custom_call" | custom-call | tf_op jit(solution)/shard_map/pallas_call | solution.py:49
  434.8 8.3 %shard_map.110 = (bf16[2,128,512]{2,1,0:T(8,128)(2,1)}, bf16[2,128,512]{2,1,0:T(8,128)(2,1)}, bf16[2,128,512]{2,1,0:T(8,128)(2,1)}, bf16[2,128,512]{2,1,0:T(8,12...) custom-call(s32[8]{0:T(128)} %and_select_fusion.1.place_ref, ...), custom_call_target="tpu_custom_call" | custom-call | tf_op jit(solution)/shard_map/pallas_call | solution.py:49
  443.1 30.5 %collective-permute-start.29 = (bf16[2,128,512]{2,1,0:T(8,128)(2,1)}, bf16[2,128,512]{2,1,0:T(8,128)(2,1)S(1)}, u32[]{:S(2)}, u32[]{:S(2)}) collective-permute-start(bf16[2,128,512]{2,1,0:T(8,128)(2,1)} %get-tuple-element.103), channel_id=1, source_target_pairs={{0,1},{1,2},{2,3},{3,4},{4,5},{5,6},{6,7},{7,0},{8,9},{9,10},{10,1... | collective-permute-start | bytes 786440 | tf_op jit(solution)/shard_map/ppermute | solution.py:687
  473.6 2.1 collective-permute-start.31
  475.7 1.4 collective-permute-start.32
  477.1 2.6 collective-permute-start.33
  479.7 2.0 collective-permute-start.34
  481.7 7.0 %collective-permute-done.30.refs_2_ = bf16[2,128,512]{2,1,0:T(8,128)(2,1)S(1)} collective-permute-done((bf16[2,128,512]{2,1,0:T(8,128)(2,1)}, bf16[2,128,512]{2,1,0:T(8,128)(2,1)S(1)}, u32[]{:S(2)}, u32[]{:S(2)}) %collective-permute-start.30) | collective-permute-done | bytes 262176 | tf_op jit(solution)/shard_map/ppermute | solution.py:687
  488.7 10.8 %collective-permute-done.31.refs_3_ = bf16[2,128,512]{2,1,0:T(8,128)(2,1)S(1)} collective-permute-done((bf16[2,128,512]{2,1,0:T(8,128)(2,1)}, bf16[2,128,512]{2,1,0:T(8,128)(2,1)S(1)}, u32[]{:S(2)}, u32[]{:S(2)}) %collective-permute-start.31) | collective-permute-done | bytes 262176 | tf_op jit(solution)/shard_map/ppermute | solution.py:687
  501.2 3.6 shard_map.111
  504.9 4.9 shard_map.112
  509.8 19.2 %all_to_all.41 = bf16[8,128,512]{2,1,0:T(8,128)(2,1)S(1)} all-to-all(bf16[8,128,512]{2,1,0:T(8,128)(2,1)} %shard_map.112), channel_id=1, replica_groups=mesh['z'=8,'x'=4,'head'=8] {'head'}, dimensions={0} | all-to-all | bytes 2097152 | tf_op jit(solution)/shard_map/all_to_all | solution.py:700
  529.7 1.3 copy.60
  (150 shorter events, 29.7 us)
Async XLA Ops:
  0.6 288.6 %copy-start = (s32[256,2]{0,1:T(2,128)S(1)}, s32[256,2]{0,1:T(2,128)}, u32[]{:S(2)}) copy-start(s32[256,2]{0,1:T(2,128)} %param.13) | copy-start | bytes 6148
  0.6 2.3 copy-start.5
  5.6 6.9 %copy-start.30 = (s32[256,3]{0,1:T(4,128)S(1)}, s32[256,3]{0,1:T(4,128)}, u32[]{:S(2)}) copy-start(s32[256,3]{0,1:T(4,128)} %param.11) | copy-start | bytes 9220
  5.6 33.2 %all-to-all-start = ((bf16[8,2,128,512]{3,2,1,0:T(8,128)(2,1)}), bf16[8,2,128,512]{3,2,1,0:T(8,128)(2,1)S(1)}, u32[]{:S(2)}, u32[]{:S(2)}) async-start(bf16[8,2,128,512]{3,2,1,0:T(8,128)(2,1)} %pad_maximum_fusion), calls=%async_computation | async-start | bytes 4194304 | tf_op jit(solution)/shard_map/all_to_all | solution.py:519
  12.8 33.3 %copy-start.32 = (s32[24]{0:T(128)}, s32[24]{0:T(128)S(1)}, u32[]{:S(2)}) copy-start(s32[24]{0:T(128)S(1)} %fusion.2.owner_ref) | copy-start | bytes 292
  38.9 1.4 copy-start.2
  46.1 212.1 %all-to-all-start.1 = ((bf16[32,2,128,512]{3,2,1,0:T(8,128)(2,1)}), bf16[32,2,128,512]{3,2,1,0:T(8,128)(2,1)}, u32[]{:S(2)}, u32[]{:S(2)}) async-start(bf16[32,2,128,512]{3,2,1,0:T(8,128)(2,1)} %shard_map.94), calls=%async_computation.1 | async-start | bytes 16777216 | tf_op jit(solution)/shard_map/all_to_all | solution.py:523
  60.8 7.5 %collective-permute-start = (bf16[2,128,512]{2,1,0:T(8,128)(2,1)}, bf16[2,128,512]{2,1,0:T(8,128)(2,1)S(1)}, u32[]{:S(2)}, u32[]{:S(2)}) collective-permute-start(bf16[2,128,512]{2,1,0:T(8,128)(2,1)} %get-tuple-element.62), channel_id=1, source_target_pairs={{0,1},{1,2},{2,3},{3,4},{4,5},{5,6},{6,7},{7,0},{8,9},{9,10},{10,1... | collective-permute-start | bytes 786440 | tf_op jit(solution)/shard_map/ppermute | solution.py:526
  62.1 15.2 %collective-permute-start.1 = (bf16[2,128,512]{2,1,0:T(8,128)(2,1)}, bf16[2,128,512]{2,1,0:T(8,128)(2,1)S(1)}, u32[]{:S(2)}, u32[]{:S(2)}) collective-permute-start(bf16[2,128,512]{2,1,0:T(8,128)(2,1)} %get-tuple-element.63), channel_id=1, source_target_pairs={{0,2},{1,3},{2,4},{3,5},{4,6},{5,7},{6,0},{7,1},{8,10},{9,11},{10,... | collective-permute-start | bytes 786440 | tf_op jit(solution)/shard_map/ppermute | solution.py:526
  62.1 26.4 %collective-permute-start.2 = (bf16[2,128,512]{2,1,0:T(8,128)(2,1)}, bf16[2,128,512]{2,1,0:T(8,128)(2,1)S(1)}, u32[]{:S(2)}, u32[]{:S(2)}) collective-permute-start(bf16[2,128,512]{2,1,0:T(8,128)(2,1)} %get-tuple-element.64), channel_id=1, source_target_pairs={{0,3},{1,4},{2,5},{3,6},{4,7},{5,0},{6,1},{7,2},{8,11},{9,12},{10,... | collective-permute-start | bytes 786440 | tf_op jit(solution)/shard_map/ppermute | solution.py:526
  64.2 24.3 %collective-permute-start.3 = (bf16[2,128,512]{2,1,0:T(8,128)(2,1)}, bf16[2,128,512]{2,1,0:T(8,128)(2,1)S(1)}, u32[]{:S(2)}, u32[]{:S(2)}) collective-permute-start(bf16[2,128,512]{2,1,0:T(8,128)(2,1)} %get-tuple-element.65), channel_id=1, source_target_pairs={{0,4},{1,5},{2,6},{3,7},{4,0},{5,1},{6,2},{7,3},{8,12},{9,13},{10,... | collective-permute-start | bytes 786440 | tf_op jit(solution)/shard_map/ppermute | solution.py:526
  65.7 22.9 %collective-permute-start.4 = (bf16[2,128,512]{2,1,0:T(8,128)(2,1)}, bf16[2,128,512]{2,1,0:T(8,128)(2,1)S(1)}, u32[]{:S(2)}, u32[]{:S(2)}) collective-permute-start(bf16[2,128,512]{2,1,0:T(8,128)(2,1)} %get-tuple-element.66), channel_id=1, source_target_pairs={{0,5},{1,6},{2,7},{3,0},{4,1},{5,2},{6,3},{7,4},{8,13},{9,14},{10,... | collective-permute-start | bytes 786440 | tf_op jit(solution)/shard_map/ppermute | solution.py:526
  68.3 21.2 %copy-start.11 = (bf16[2,128,512]{2,1,0:T(8,128)(2,1)}, bf16[2,128,512]{2,1,0:T(8,128)(2,1)S(1)}, u32[]{:S(2)}) copy-start(bf16[2,128,512]{2,1,0:T(8,128)(2,1)S(1)} %collective-permute-done.refs_1_) | copy-start | bytes 786436
  68.3 20.3 %collective-permute-start.5 = (bf16[2,128,512]{2,1,0:T(8,128)(2,1)}, bf16[2,128,512]{2,1,0:T(8,128)(2,1)S(1)}, u32[]{:S(2)}, u32[]{:S(2)}) collective-permute-start(bf16[2,128,512]{2,1,0:T(8,128)(2,1)} %get-tuple-element.67), channel_id=1, source_target_pairs={{0,6},{1,7},{2,0},{3,1},{4,2},{5,3},{6,4},{7,5},{8,14},{9,15},{10,... | collective-permute-start | bytes 786440 | tf_op jit(solution)/shard_map/ppermute | solution.py:526
  77.3 12.2 %copy-start.13 = (bf16[2,128,512]{2,1,0:T(8,128)(2,1)}, bf16[2,128,512]{2,1,0:T(8,128)(2,1)S(1)}, u32[]{:S(2)}) copy-start(bf16[2,128,512]{2,1,0:T(8,128)(2,1)S(1)} %collective-permute-done.1.refs_2_) | copy-start | bytes 786436
  77.3 12.2 %collective-permute-start.6 = (bf16[2,128,512]{2,1,0:T(8,128)(2,1)}, bf16[2,128,512]{2,1,0:T(8,128)(2,1)S(1)}, u32[]{:S(2)}, u32[]{:S(2)}) collective-permute-start(bf16[2,128,512]{2,1,0:T(8,128)(2,1)} %get-tuple-element.68), channel_id=1, source_target_pairs={{0,7},{1,0},{2,1},{3,2},{4,3},{5,4},{6,5},{7,6},{8,15},{9,8},{10,9... | collective-permute-start | bytes 786440 | tf_op jit(solution)/shard_map/ppermute | solution.py:526
  88.5 1.0 copy-start.15
  88.5 1.0 copy-start.17
  88.5 1.0 copy-start.20
  88.6 0.9 copy-start.26
  93.8 163.6 %copy-start.31 = (s32[256,3]{0,1:T(4,128)S(1)}, s32[256,3]{0,1:T(4,128)}, u32[]{:S(2)}) copy-start(s32[256,3]{0,1:T(4,128)} %param.12) | copy-start | bytes 9220
  95.2 21.6 %collective-permute-start.10 = (bf16[2,128,512]{2,1,0:T(8,128)(2,1)S(1)}, bf16[2,128,512]{2,1,0:T(8,128)(2,1)S(1)}, u32[]{:S(2)}, u32[]{:S(2)}) collective-permute-start(bf16[2,128,512]{2,1,0:T(8,128)(2,1)S(1)} %get-tuple-element.130), channel_id=1, source_target_pairs={{0,16},{1,17},{2,18},{3,19},{4,20},{5,21},{6,22},{7,23}} | collective-permute-start | bytes 786440 | tf_op jit(solution)/shard_map/ppermute | solution.py:533
  100.1 38.6 %collective-permute-start.11 = (bf16[2,128,512]{2,1,0:T(8,128)(2,1)S(1)}, bf16[2,128,512]{2,1,0:T(8,128)(2,1)S(1)}, u32[]{:S(2)}, u32[]{:S(2)}) collective-permute-start(bf16[2,128,512]{2,1,0:T(8,128)(2,1)S(1)} %get-tuple-element.129), channel_id=1, source_target_pairs={{0,8},{1,9},{2,10},{3,11},{4,12},{5,13},{6,14},{7,15}} | collective-permute-start | bytes 786440 | tf_op jit(solution)/shard_map/ppermute | solution.py:533
  101.4 37.3 %collective-permute-start.9 = (bf16[2,128,512]{2,1,0:T(8,128)(2,1)S(1)}, bf16[2,128,512]{2,1,0:T(8,128)(2,1)S(1)}, u32[]{:S(2)}, u32[]{:S(2)}) collective-permute-start(bf16[2,128,512]{2,1,0:T(8,128)(2,1)S(1)} %get-tuple-element.131), channel_id=1, source_target_pairs={{0,24},{1,25},{2,26},{3,27},{4,28},{5,29},{6,30},{7,31}} | collective-permute-start | bytes 786440 | tf_op jit(solution)/shard_map/ppermute | solution.py:533
  139.7 106.0 %collective-permute-start.12 = (bf16[2,128,512]{2,1,0:T(8,128)(2,1)S(1)}, bf16[2,128,512]{2,1,0:T(8,128)(2,1)S(1)}, u32[]{:S(2)}, u32[]{:S(2)}) collective-permute-start(bf16[2,128,512]{2,1,0:T(8,128)(2,1)S(1)} %select_select_fusion), channel_id=1, source_target_pairs={{0,128},{1,129},{2,130},{3,131},{4,132},{5,133},{6,134},{7,135},{8... | collective-permute-start | bytes 786440 | tf_op jit(solution)/shard_map/ppermute | solution.py:538
  245.7 5.4 %collective-permute-start.13 = (bf16[2,128,512]{2,1,0:T(8,128)(2,1)S(1)}, bf16[2,128,512]{2,1,0:T(8,128)(2,1)S(1)}, u32[]{:S(2)}, u32[]{:S(2)}) collective-permute-start(bf16[2,128,512]{2,1,0:T(8,128)(2,1)S(1)} %broadcast_select_fusion), channel_id=1, source_target_pairs={{0,64},{128,192},{1,65},{129,193},{2,66},{130,194},{3,67},{131,195... | collective-permute-start | bytes 786440 | tf_op jit(solution)/shard_map/ppermute | solution.py:538
  251.2 7.0 %collective-permute-start.14 = (bf16[2,128,512]{2,1,0:T(8,128)(2,1)S(1)}, bf16[2,128,512]{2,1,0:T(8,128)(2,1)S(1)}, u32[]{:S(2)}, u32[]{:S(2)}) collective-permute-start(bf16[2,128,512]{2,1,0:T(8,128)(2,1)S(1)} %broadcast_select_fusion.1), channel_id=1, source_target_pairs={{0,32},{64,96},{128,160},{192,224},{1,33},{65,97},{129,161},{193,2... | collective-permute-start | bytes 786440 | tf_op jit(solution)/shard_map/ppermute | solution.py:538
  252.5 17.3 %collective-permute-start.7 = (bf16[2,128,512]{2,1,0:T(8,128)(2,1)S(1)}, bf16[2,128,512]{2,1,0:T(8,128)(2,1)S(1)}, u32[]{:S(2)}, u32[]{:S(2)}) collective-permute-start(bf16[2,128,512]{2,1,0:T(8,128)(2,1)S(1)} %get-tuple-element.133), channel_id=1, source_target_pairs={{0,8},{8,16},{16,24},{24,32},{32,40},{40,48},{48,56},{56,64},{64,7... | collective-permute-start | bytes 786440 | tf_op jit(solution)/shard_map/ppermute | solution.py:528
  252.6 17.2 %collective-permute-start.8 = (bf16[2,128,512]{2,1,0:T(8,128)(2,1)S(1)}, bf16[2,128,512]{2,1,0:T(8,128)(2,1)S(1)}, u32[]{:S(2)}, u32[]{:S(2)}) collective-permute-start(bf16[2,128,512]{2,1,0:T(8,128)(2,1)S(1)} %get-tuple-element.132), channel_id=1, source_target_pairs={{8,0},{16,8},{24,16},{32,24},{40,32},{48,40},{56,48},{64,56},{72,6... | collective-permute-start | bytes 786440 | tf_op jit(solution)/shard_map/ppermute | solution.py:529
  258.2 19.9 %copy-start.6 = (bf16[2,128,512]{2,1,0:T(8,128)(2,1)}, bf16[2,128,512]{2,1,0:T(8,128)(2,1)S(1)}, u32[]{:S(2)}) copy-start(bf16[2,128,512]{2,1,0:T(8,128)(2,1)S(1)} %broadcast_select_fusion.2.refs_0_) | copy-start | bytes 786436
  269.7 21.4 %copy-start.3 = (bf16[2,128,512]{2,1,0:T(8,128)(2,1)}, bf16[2,128,512]{2,1,0:T(8,128)(2,1)S(1)}, u32[]{:S(2)}) copy-start(bf16[2,128,512]{2,1,0:T(8,128)(2,1)S(1)} %collective-permute-done.7.left_ref) | copy-start | bytes 786436
  269.7 21.4 %copy-start.4 = (bf16[2,128,512]{2,1,0:T(8,128)(2,1)}, bf16[2,128,512]{2,1,0:T(8,128)(2,1)S(1)}, u32[]{:S(2)}) copy-start(bf16[2,128,512]{2,1,0:T(8,128)(2,1)S(1)} %collective-permute-done.8.right_ref) | copy-start | bytes 786436
  269.8 9.5 %all-to-all-start.2 = ((f32[4,8,8,128]{3,2,1,0:T(8,128)}), f32[4,8,8,128]{3,2,1,0:T(8,128)S(1)}, u32[]{:S(2)}, u32[]{:S(2)}) async-start(f32[4,8,8,128]{3,2,1,0:T(8,128)} %bitcast.53), calls=%async_computation.2 | async-start | bytes 262144 | tf_op jit(solution)/shard_map/all_to_all | solution.py:469
  274.3 28.9 %collective-permute-start.15 = (bf16[2,128,512]{2,1,0:T(8,128)(2,1)S(1)}, bf16[2,128,512]{2,1,0:T(8,128)(2,1)S(1)}, u32[]{:S(2)}, u32[]{:S(2)}) collective-permute-start(bf16[2,128,512]{2,1,0:T(8,128)(2,1)S(1)} %broadcast_select_fusion.2.refs_0_), channel_id=1, source_target_pairs={{0,8},{8,16},{16,24},{24,0},{1,9},{9,17},{17,25},{25,1},{2,10},{10... | collective-permute-start | bytes 786440 | tf_op jit(solution)/shard_map/ppermute | solution.py:557
  275.7 27.4 %collective-permute-start.16 = (bf16[2,128,512]{2,1,0:T(8,128)(2,1)S(1)}, bf16[2,128,512]{2,1,0:T(8,128)(2,1)S(1)}, u32[]{:S(2)}, u32[]{:S(2)}) collective-permute-start(bf16[2,128,512]{2,1,0:T(8,128)(2,1)S(1)} %broadcast_select_fusion.2.refs_0_), channel_id=1, source_target_pairs={{0,16},{8,24},{16,0},{24,8},{1,17},{9,25},{17,1},{25,9},{2,18},{10... | collective-permute-start | bytes 786440 | tf_op jit(solution)/shard_map/ppermute | solution.py:557
  278.1 25.0 %collective-permute-start.17 = (bf16[2,128,512]{2,1,0:T(8,128)(2,1)S(1)}, bf16[2,128,512]{2,1,0:T(8,128)(2,1)S(1)}, u32[]{:S(2)}, u32[]{:S(2)}) collective-permute-start(bf16[2,128,512]{2,1,0:T(8,128)(2,1)S(1)} %broadcast_select_fusion.2.refs_0_), channel_id=1, source_target_pairs={{0,24},{8,0},{16,8},{24,16},{1,25},{9,1},{17,9},{25,17},{2,26},{10... | collective-permute-start | bytes 786440 | tf_op jit(solution)/shard_map/ppermute | solution.py:557
  280.0 35.2 %all-to-all-start.3 = ((f32[4,8,8,128]{3,2,0,1:T(8,128)}), f32[4,8,8,128]{3,2,0,1:T(8,128)S(1)}, u32[]{:S(2)}, u32[]{:S(2)}) async-start(f32[4,8,8,128]{3,2,0,1:T(8,128)} %copy.55), calls=%async_computation.3 | async-start | bytes 262144 | tf_op jit(solution)/shard_map/all_to_all | solution.py:470
  327.0 17.9 %all-to-all-start.5 = ((f32[4,8,8,128]{3,2,0,1:T(8,128)}), f32[4,8,8,128]{3,2,0,1:T(8,128)S(1)}, u32[]{:S(2)}, u32[]{:S(2)}) async-start(f32[4,8,8,128]{3,2,0,1:T(8,128)} %copy.57), calls=%async_computation.5 | async-start | bytes 262144 | tf_op jit(solution)/shard_map/all_to_all | solution.py:470
  347.0 9.7 %collective-permute-start.18 = (bf16[2,128,512]{2,1,0:T(8,128)(2,1)S(1)}, bf16[2,128,512]{2,1,0:T(8,128)(2,1)S(1)}, u32[]{:S(2)}, u32[]{:S(2)}) collective-permute-start(bf16[2,128,512]{2,1,0:T(8,128)(2,1)S(1)} %get-tuple-element.138), channel_id=1, source_target_pairs={{0,8},{8,16},{16,24},{24,0},{1,9},{9,17},{17,25},{25,1},{2,10},{10... | collective-permute-start | bytes 786440 | tf_op jit(solution)/shard_map/ppermute | solution.py:607
  347.3 9.4 %collective-permute-start.19 = (bf16[2,128,512]{2,1,0:T(8,128)(2,1)S(1)}, bf16[2,128,512]{2,1,0:T(8,128)(2,1)S(1)}, u32[]{:S(2)}, u32[]{:S(2)}) collective-permute-start(bf16[2,128,512]{2,1,0:T(8,128)(2,1)S(1)} %get-tuple-element.137), channel_id=1, source_target_pairs={{0,16},{8,24},{16,0},{24,8},{1,17},{9,25},{17,1},{25,9},{2,18},{10... | collective-permute-start | bytes 786440 | tf_op jit(solution)/shard_map/ppermute | solution.py:607
  349.1 7.8 %collective-permute-start.20 = (bf16[2,128,512]{2,1,0:T(8,128)(2,1)S(1)}, bf16[2,128,512]{2,1,0:T(8,128)(2,1)S(1)}, u32[]{:S(2)}, u32[]{:S(2)}) collective-permute-start(bf16[2,128,512]{2,1,0:T(8,128)(2,1)S(1)} %get-tuple-element.136), channel_id=1, source_target_pairs={{0,24},{8,0},{16,8},{24,16},{1,25},{9,1},{17,9},{25,17},{2,26},{10... | collective-permute-start | bytes 786440 | tf_op jit(solution)/shard_map/ppermute | solution.py:607
  358.1 7.5 %collective-permute-start.21 = (bf16[2,128,512]{2,1,0:T(8,128)(2,1)S(1)}, bf16[2,128,512]{2,1,0:T(8,128)(2,1)S(1)}, u32[]{:S(2)}, u32[]{:S(2)}) collective-permute-start(bf16[2,128,512]{2,1,0:T(8,128)(2,1)S(1)} %convert_element_type.49), channel_id=1, source_target_pairs={{32,0},{96,64},{160,128},{224,192},{33,1},{97,65},{161,129},{225,1... | collective-permute-start | bytes 786440 | tf_op jit(solution)/shard_map/ppermute | solution.py:649
  365.7 8.0 %collective-permute-start.22 = (bf16[2,128,512]{2,1,0:T(8,128)(2,1)S(1)}, bf16[2,128,512]{2,1,0:T(8,128)(2,1)S(1)}, u32[]{:S(2)}, u32[]{:S(2)}) collective-permute-start(bf16[2,128,512]{2,1,0:T(8,128)(2,1)S(1)} %convert_element_type.51), channel_id=1, source_target_pairs={{64,0},{192,128},{65,1},{193,129},{66,2},{194,130},{67,3},{195,131... | collective-permute-start | bytes 786440 | tf_op jit(solution)/shard_map/ppermute | solution.py:649
  373.9 12.3 %collective-permute-start.23 = (bf16[2,128,512]{2,1,0:T(8,128)(2,1)S(1)}, bf16[2,128,512]{2,1,0:T(8,128)(2,1)S(1)}, u32[]{:S(2)}, u32[]{:S(2)}) collective-permute-start(bf16[2,128,512]{2,1,0:T(8,128)(2,1)S(1)} %convert_element_type.53), channel_id=1, source_target_pairs={{128,0},{129,1},{130,2},{131,3},{132,4},{133,5},{134,6},{135,7},{1... | collective-permute-start | bytes 786440 | tf_op jit(solution)/shard_map/ppermute | solution.py:649
  375.2 11.1 %collective-permute-start.24 = (bf16[2,128,512]{2,1,0:T(8,128)(2,1)S(1)}, bf16[2,128,512]{2,1,0:T(8,128)(2,1)S(1)}, u32[]{:S(2)}, u32[]{:S(2)}) collective-permute-start(bf16[2,128,512]{2,1,0:T(8,128)(2,1)S(1)} %get-tuple-element.135), channel_id=1, source_target_pairs={{0,8},{8,16},{16,24},{24,32},{32,40},{40,48},{48,56},{56,64},{64,7... | collective-permute-start | bytes 786440 | tf_op jit(solution)/shard_map/ppermute | solution.py:602
  375.9 10.5 %collective-permute-start.25 = (bf16[2,128,512]{2,1,0:T(8,128)(2,1)S(1)}, bf16[2,128,512]{2,1,0:T(8,128)(2,1)S(1)}, u32[]{:S(2)}, u32[]{:S(2)}) collective-permute-start(bf16[2,128,512]{2,1,0:T(8,128)(2,1)S(1)} %get-tuple-element.134), channel_id=1, source_target_pairs={{8,0},{16,8},{24,16},{32,24},{40,32},{48,40},{56,48},{64,56},{72,6... | collective-permute-start | bytes 786440 | tf_op jit(solution)/shard_map/ppermute | solution.py:603
  386.3 11.3 %copy-start.7 = (bf16[2,128,512]{2,1,0:T(8,128)(2,1)}, bf16[2,128,512]{2,1,0:T(8,128)(2,1)S(1)}, u32[]{:S(2)}) copy-start(bf16[2,128,512]{2,1,0:T(8,128)(2,1)S(1)} %convert_add_fusion.1.refs_3_) | copy-start | bytes 786436
  387.2 117.7 %all-to-all-start.6 = ((bf16[32,128,512]{2,1,0:T(8,128)(2,1)}), bf16[32,128,512]{2,1,0:T(8,128)(2,1)}, u32[]{:S(2)}, u32[]{:S(2)}) async-start(bf16[32,128,512]{2,1,0:T(8,128)(2,1)} %get-tuple-element.96), calls=%async_computation.6 | async-start | bytes 8388608 | tf_op jit(solution)/shard_map/all_to_all | solution.py:654
  395.0 38.9 %collective-permute-start.26 = (bf16[2,128,512]{2,1,0:T(8,128)(2,1)S(1)}, bf16[2,128,512]{2,1,0:T(8,128)(2,1)S(1)}, u32[]{:S(2)}, u32[]{:S(2)}) collective-permute-start(bf16[2,128,512]{2,1,0:T(8,128)(2,1)S(1)} %convert_add_fusion.1.refs_3_), channel_id=1, source_target_pairs={{8,0},{9,1},{10,2},{11,3},{12,4},{13,5},{14,6},{15,7}} | collective-permute-start | bytes 786440 | tf_op jit(solution)/shard_map/ppermute | solution.py:666
  396.3 37.6 %collective-permute-start.27 = (bf16[2,128,512]{2,1,0:T(8,128)(2,1)S(1)}, bf16[2,128,512]{2,1,0:T(8,128)(2,1)S(1)}, u32[]{:S(2)}, u32[]{:S(2)}) collective-permute-start(bf16[2,128,512]{2,1,0:T(8,128)(2,1)S(1)} %convert_add_fusion.1.refs_3_), channel_id=1, source_target_pairs={{16,0},{17,1},{18,2},{19,3},{20,4},{21,5},{22,6},{23,7}} | collective-permute-start | bytes 786440 | tf_op jit(solution)/shard_map/ppermute | solution.py:666
  397.6 36.4 %collective-permute-start.28 = (bf16[2,128,512]{2,1,0:T(8,128)(2,1)S(1)}, bf16[2,128,512]{2,1,0:T(8,128)(2,1)S(1)}, u32[]{:S(2)}, u32[]{:S(2)}) collective-permute-start(bf16[2,128,512]{2,1,0:T(8,128)(2,1)S(1)} %convert_add_fusion.1.refs_3_), channel_id=1, source_target_pairs={{24,0},{25,1},{26,2},{27,3},{28,4},{29,5},{30,6},{31,7}} | collective-permute-start | bytes 786440 | tf_op jit(solution)/shard_map/ppermute | solution.py:666
  443.1 36.6 %collective-permute-start.29 = (bf16[2,128,512]{2,1,0:T(8,128)(2,1)}, bf16[2,128,512]{2,1,0:T(8,128)(2,1)S(1)}, u32[]{:S(2)}, u32[]{:S(2)}) collective-permute-start(bf16[2,128,512]{2,1,0:T(8,128)(2,1)} %get-tuple-element.103), channel_id=1, source_target_pairs={{0,1},{1,2},{2,3},{3,4},{4,5},{5,6},{6,7},{7,0},{8,9},{9,10},{10,1... | collective-permute-start | bytes 786440 | tf_op jit(solution)/shard_map/ppermute | solution.py:687
  473.6 15.1 %collective-permute-start.30 = (bf16[2,128,512]{2,1,0:T(8,128)(2,1)}, bf16[2,128,512]{2,1,0:T(8,128)(2,1)S(1)}, u32[]{:S(2)}, u32[]{:S(2)}) collective-permute-start(bf16[2,128,512]{2,1,0:T(8,128)(2,1)} %get-tuple-element.104), channel_id=1, source_target_pairs={{0,2},{1,3},{2,4},{3,5},{4,6},{5,7},{6,0},{7,1},{8,10},{9,11},{10,... | collective-permute-start | bytes 786440 | tf_op jit(solution)/shard_map/ppermute | solution.py:687
  473.6 26.0 %collective-permute-start.31 = (bf16[2,128,512]{2,1,0:T(8,128)(2,1)}, bf16[2,128,512]{2,1,0:T(8,128)(2,1)S(1)}, u32[]{:S(2)}, u32[]{:S(2)}) collective-permute-start(bf16[2,128,512]{2,1,0:T(8,128)(2,1)} %get-tuple-element.105), channel_id=1, source_target_pairs={{0,3},{1,4},{2,5},{3,6},{4,7},{5,0},{6,1},{7,2},{8,11},{9,12},{10,... | collective-permute-start | bytes 786440 | tf_op jit(solution)/shard_map/ppermute | solution.py:687
  475.7 23.9 %collective-permute-start.32 = (bf16[2,128,512]{2,1,0:T(8,128)(2,1)}, bf16[2,128,512]{2,1,0:T(8,128)(2,1)S(1)}, u32[]{:S(2)}, u32[]{:S(2)}) collective-permute-start(bf16[2,128,512]{2,1,0:T(8,128)(2,1)} %get-tuple-element.106), channel_id=1, source_target_pairs={{0,4},{1,5},{2,6},{3,7},{4,0},{5,1},{6,2},{7,3},{8,12},{9,13},{10,... | collective-permute-start | bytes 786440 | tf_op jit(solution)/shard_map/ppermute | solution.py:687
  477.1 22.5 %collective-permute-start.33 = (bf16[2,128,512]{2,1,0:T(8,128)(2,1)}, bf16[2,128,512]{2,1,0:T(8,128)(2,1)S(1)}, u32[]{:S(2)}, u32[]{:S(2)}) collective-permute-start(bf16[2,128,512]{2,1,0:T(8,128)(2,1)} %get-tuple-element.107), channel_id=1, source_target_pairs={{0,5},{1,6},{2,7},{3,0},{4,1},{5,2},{6,3},{7,4},{8,13},{9,14},{10,... | collective-permute-start | bytes 786440 | tf_op jit(solution)/shard_map/ppermute | solution.py:687
  479.7 20.8 %copy-start.10 = (bf16[2,128,512]{2,1,0:T(8,128)(2,1)}, bf16[2,128,512]{2,1,0:T(8,128)(2,1)S(1)}, u32[]{:S(2)}) copy-start(bf16[2,128,512]{2,1,0:T(8,128)(2,1)S(1)} %collective-permute-done.29.refs_1_) | copy-start | bytes 786436
  479.7 20.1 %collective-permute-start.34 = (bf16[2,128,512]{2,1,0:T(8,128)(2,1)}, bf16[2,128,512]{2,1,0:T(8,128)(2,1)S(1)}, u32[]{:S(2)}, u32[]{:S(2)}) collective-permute-start(bf16[2,128,512]{2,1,0:T(8,128)(2,1)} %get-tuple-element.108), channel_id=1, source_target_pairs={{0,6},{1,7},{2,0},{3,1},{4,2},{5,3},{6,4},{7,5},{8,14},{9,15},{10,... | collective-permute-start | bytes 786440 | tf_op jit(solution)/shard_map/ppermute | solution.py:687
  488.7 11.9 %copy-start.12 = (bf16[2,128,512]{2,1,0:T(8,128)(2,1)}, bf16[2,128,512]{2,1,0:T(8,128)(2,1)S(1)}, u32[]{:S(2)}) copy-start(bf16[2,128,512]{2,1,0:T(8,128)(2,1)S(1)} %collective-permute-done.30.refs_2_) | copy-start | bytes 786436
  488.7 11.9 %collective-permute-start.35 = (bf16[2,128,512]{2,1,0:T(8,128)(2,1)}, bf16[2,128,512]{2,1,0:T(8,128)(2,1)S(1)}, u32[]{:S(2)}, u32[]{:S(2)}) collective-permute-start(bf16[2,128,512]{2,1,0:T(8,128)(2,1)} %get-tuple-element.109), channel_id=1, source_target_pairs={{0,7},{1,0},{2,1},{3,2},{4,3},{5,4},{6,5},{7,6},{8,15},{9,8},{10,9... | collective-permute-start | bytes 786440 | tf_op jit(solution)/shard_map/ppermute | solution.py:687
  499.5 1.0 copy-start.14
  499.5 1.0 copy-start.16
  499.5 1.0 copy-start.19
  509.8 21.2 %copy-start.1 = (s32[256,2]{0,1:T(2,128)S(1)}, s32[256,2]{0,1:T(2,128)}, u32[]{:S(2)}) copy-start(s32[256,2]{0,1:T(2,128)} %param.13) | copy-start | bytes 6148
  (11 other events, 8.3 us)
